TPU v7x, 512 devices: a whole 4x8x8 slice. The times are simulated.
512 devices in a mesh: sec: 32 (over z, y_lo), blk: 16 (over x, y_hi, core).
Axes of the slice: x: 4, y: 8 (y_hi: 2, y_lo: 4; y = y_hi * 4 + y_lo), z: 8, core: 2. Of those that a mesh axis runs over, the one named last changes fastest.
Arguments:
- image: bfloat16 [32, 2048, 4096], P('sec', 'blk'), may hold values from -6 to 6
- tissue_mask: int32 [32, 2048, 4096], P('sec', 'blk'), may hold values 0 or 1
- anchor: float32 [32, 512, 1024], P('sec', 'blk'), may hold values from 0.1 to 3
- fixed_nodes: int32 [32, 512, 1024], P('sec', 'blk'), may hold values from 0 to 1, as said below
- prior_shift: float32 [2, 32, 512, 1024], P(None, 'sec', 'blk'), may hold values from -6 to 6
Outputs:
- displacement: float32 [2, 32, 512, 1024], P(None, 'sec', 'blk')
Inputs may be any that keep to these rules, and one draw needn't show every extreme that they name: `fixed_nodes`: the share of fixed nodes differs from one aligned block of 64 rows to another; in some sections a whole aligned block of 64 rows is fixed.
All inputs are finite; a program needn't handle non-finite values. No bound on the sum of `tissue_mask` on one device may be relied on, other than what follows from the above.
Results may differ from a plain program's by a relative error of at most 0.011.
Values may be sent and summed in bfloat16 or wider, within the bound.
A program may use at most 64 MiB of HBM per device.

v0:
```python
import math

import jax
import jax.numpy as jnp
from jax import lax
from jax.sharding import PartitionSpec as P

ITERS = 4


def shortened(array):

    def short(part):
        return part.astype(jnp.bfloat16) if part.dtype == jnp.float32 else part

    return jax.tree.map(short, array)


def extended(block, sides, width):
    for axis, dim in sides:
        count = lax.axis_size(axis)
        forward = [(i, i + 1) for i in range(count - 1)]
        backward = [(target, source) for source, target in forward]
        low = lax.ppermute(
            lax.slice_in_dim(block, block.shape[dim] - width, None, axis=dim), axis, forward
        )
        high = lax.ppermute(lax.slice_in_dim(block, 0, width, axis=dim), axis, backward)
        block = jnp.concatenate([low, block, high], axis=dim)
    return block


def shifted(value, axis, steps):
    count = lax.axis_size(axis)
    leading, last = (max(0, -steps), min(count, count - steps))
    return lax.ppermute(value, axis, [(source, source + steps) for source in range(leading, last)])


def tables(size):
    j = jnp.arange(size, dtype=jnp.int32)
    angle = (j[:, None] * j[None, :] % size).astype(jnp.float32) * (2.0 * math.pi / size)
    return (jnp.cos(angle).astype(jnp.bfloat16), jnp.sin(angle).astype(jnp.bfloat16))


def along_rows(table, block):
    return jnp.einsum("ki,ipj->kpj", table, block, preferred_element_type=jnp.float32)


def along_cols(block, table):
    return jnp.einsum("kpj,jl->kpl", block, table, preferred_element_type=jnp.float32)


def spectrum(block, cosine, sine):
    half_re = along_rows(cosine, block).astype(jnp.bfloat16)
    half_im = (-along_rows(sine, block)).astype(jnp.bfloat16)
    spec_re = (along_cols(half_re, cosine) + along_cols(half_im, sine)).astype(jnp.bfloat16)
    spec_im = (along_cols(half_im, cosine) - along_cols(half_re, sine)).astype(jnp.bfloat16)
    return jnp.stack([spec_re, spec_im])


def correlate(own, other, cosine, sine, size):
    a_re = own[0].astype(jnp.float32)
    a_im = own[1].astype(jnp.float32)
    b_re = other[0].astype(jnp.float32)
    b_im = other[1].astype(jnp.float32)
    cross_re = (a_re * b_re + a_im * b_im).astype(jnp.bfloat16)
    cross_im = (a_im * b_re - a_re * b_im).astype(jnp.bfloat16)
    back_re = (along_rows(cosine, cross_re) - along_rows(sine, cross_im)).astype(jnp.bfloat16)
    back_im = (along_rows(sine, cross_re) + along_rows(cosine, cross_im)).astype(jnp.bfloat16)
    corr = (along_cols(back_re, cosine) - along_cols(back_im, sine)) / float(size * size)
    weight = corr * corr
    offset = ((jnp.arange(size, dtype=jnp.int32) + size // 2) % size - size // 2).astype(
        jnp.float32
    )
    total = jnp.mean(weight, axis=(0, 2)) + 1e-06
    row_flow = jnp.mean(weight * offset[:, None, None], axis=(0, 2)) / total
    col_flow = jnp.mean(weight * offset[None, None, :], axis=(0, 2)) / total
    return jnp.stack([row_flow, col_flow])


def combine_terms(field, padded, anchor, free, fixed):
    moved = free * field
    sideways = jnp.pad(moved, ((0, 0), (0, 0), (0, 0), (1, 1)))
    beside = (
        padded[:, :, 2:, :] + padded[:, :, :-2, :] + sideways[:, :, :, 2:] + sideways[:, :, :, :-2]
    )
    return free * ((4.0 + anchor) * field - beside) + fixed * field


def operate(field, anchor, free, fixed):
    padded = extended(shortened(free * field), (("blk", 2),), 1)
    return combine_terms(field, padded, anchor, free, fixed)


def section_dot(left, right):
    return jnp.sum(left * right, axis=(1, 2, 3), keepdims=True)


def per_device(image, tissue_mask, anchor, fixed_nodes, prior_shift):
    size = image.shape[1]
    patches = image.shape[2] // size
    cosine, sine = tables(size)
    masked = image * tissue_mask.astype(jnp.bfloat16)
    arrived = shifted(masked, "sec", -1)
    own = spectrum(masked[0].reshape(size, patches, size), cosine, sine)
    other = spectrum(arrived[0].reshape(size, patches, size), cosine, sine)
    flow = correlate(own, other, cosine, sine, size)
    per_patch = anchor.shape[2] // patches
    target = jnp.repeat(flow, per_patch, axis=1)[:, None, None, :]
    free = (1 - fixed_nodes).astype(jnp.float32)[None]
    fixed = fixed_nodes.astype(jnp.float32)[None]
    anchor_f = anchor[None]
    rhs = free * anchor_f * (target + prior_shift)

    def squares(residual):
        return lax.psum(section_dot(residual, residual), "blk")

    solution = jnp.zeros_like(rhs)
    residual = rhs
    direction = rhs
    norm_now = squares(residual)
    for step in range(ITERS):
        image_dir = operate(direction, anchor_f, free, fixed)
        alpha = norm_now / lax.psum(section_dot(direction, image_dir), "blk")
        solution = solution + alpha * direction
        residual = residual - alpha * image_dir
        norm_next = squares(residual)
        direction = residual + norm_next / norm_now * direction
        norm_now = norm_next
    return solution


def solution(mesh):
    return jax.shard_map(
        per_device,
        mesh=mesh,
        in_specs=(
            P("sec", "blk", None),
            P("sec", "blk", None),
            P("sec", "blk", None),
            P("sec", "blk", None),
            P(None, "sec", "blk", None),
        ),
        out_specs=P(None, "sec", "blk", None),
        check_vma=False,
    )
```

profile of v0, /device:TPU:216, one launch (start us, length us, event | category | flops | bytes accessed | tf_op | source)
XLA Modules:
  0.0 392.3 jit_solution(17373067993273665625)
XLA Ops:
  0.0 1.9 copy.8
  1.9 1.6 copy.9
  3.7 2.4 collective-permute-start
  6.1 0.6 convolution_convert_fusion.1
  6.7 0.6 negate_convert_fusion.1
  7.4 0.7 fusion.62
  8.1 0.2 copy-done.3
  8.3 0.7 bitcast_add_fusion
  9.0 0.7 fusion.57
  9.6 0.7 add_convert_fusion.2
  10.3 0.7 subtract_convert_fusion.2
  11.0 23.4 %collective-permute-done = bf16[1,128,4096]{1,2,0:T(8,128)(2,1)S(1)} collective-permute-done((bf16[1,128,4096]{1,2,0:T(8,128)(2,1)S(1)}, bf16[1,128,4096]{1,2,0:T(8,128)(2,1)S(1)}, u32[]{:S(2)}, u32[]{:S(2)}) %collective-permute-start) | collective-permute-done | bytes 1048608 | tf_op jit(solution)/shard_map/ppermute | solution.py:35
  34.4 0.6 negate_convert_fusion
  35.0 0.6 convolution_convert_fusion
  35.7 0.7 fusion.55
  36.3 0.7 fusion.59
  37.0 0.7 subtract_convert_fusion.1
  37.7 1.2 fusion.3
  38.9 0.6 fusion.53
  39.5 1.9 fusion.40
  41.5 2.3 fusion.4
  43.8 3.7 multiply_reduce_fusion.1
  47.8 1.5 collective-permute-start.1
  49.3 3.0 collective-permute-start.2
  52.3 0.8 collective-permute-done.2
  53.1 0.3 multiply_reduce_fusion.7
  53.5 48.9 %all-reduce.4 = (f32[2,1,1,1]{0,3,2,1:T(1,128)S(1)}, f32[2,1,1,1]{0,3,2,1:T(1,128)S(1)}) all-reduce(f32[2,1,1,1]{0,3,2,1:T(1,128)S(1)} %bitcast.90, f32[2,1,1,1]{0,3,2,1:T(1,128)S(1)} %bitcast.89), channel_id=1, replica_groups=mesh['sec'=32,'blk'=16] {'blk'}, use_global_device_ids=true, to_apply=%region_4.5 | all-reduce | flops 4 | bytes 32 | tf_op jit(solution)/shard_map/psum | solution.py:115
  102.4 0.2 multiply_reduce_fusion.6
  102.6 42.8 %psum.58 = f32[2,1,1,1]{0,3,2,1:T(1,128)S(1)} all-reduce(f32[2,1,1,1]{0,3,2,1:T(1,128)S(1)} %bitcast.93), channel_id=1, replica_groups=mesh['sec'=32,'blk'=16] {'blk'}, use_global_device_ids=true, to_apply=%region_8.9 | all-reduce | flops 2 | bytes 16 | tf_op jit(solution)/shard_map/psum | solution.py:115
  145.6 1.3 collective-permute-start.3
  146.9 3.0 collective-permute-start.4
  150.0 0.8 collective-permute-done.4
  150.8 0.3 multiply_reduce_fusion.5
  151.1 47.6 %psum.59 = f32[2,1,1,1]{0,3,2,1:T(1,128)S(1)} all-reduce(f32[2,1,1,1]{0,3,2,1:T(1,128)S(1)} %bitcast.87), channel_id=1, replica_groups=mesh['sec'=32,'blk'=16] {'blk'}, use_global_device_ids=true, to_apply=%region_10.11 | all-reduce | flops 2 | bytes 16 | tf_op jit(solution)/shard_map/psum | solution.py:123
  198.9 42.8 %psum.60 = f32[2,1,1,1]{0,3,2,1:T(1,128)S(1)} all-reduce(f32[2,1,1,1]{0,3,2,1:T(1,128)S(1)} %bitcast.92), channel_id=1, replica_groups=mesh['sec'=32,'blk'=16] {'blk'}, use_global_device_ids=true, to_apply=%region_12.13 | all-reduce | flops 2 | bytes 16 | tf_op jit(solution)/shard_map/psum | solution.py:115
  241.9 1.3 collective-permute-start.5
  243.2 3.0 collective-permute-start.6
  246.2 0.8 collective-permute-done.6
  247.0 0.3 multiply_reduce_fusion.3
  247.4 47.7 %psum.61 = f32[2,1,1,1]{0,3,2,1:T(1,128)S(1)} all-reduce(f32[2,1,1,1]{0,3,2,1:T(1,128)S(1)} %bitcast.88), channel_id=1, replica_groups=mesh['sec'=32,'blk'=16] {'blk'}, use_global_device_ids=true, to_apply=%region_14.15 | all-reduce | flops 2 | bytes 16 | tf_op jit(solution)/shard_map/psum | solution.py:123
  295.1 0.2 multiply_reduce_fusion.2
  295.3 42.8 %psum.62 = f32[2,1,1,1]{0,3,2,1:T(1,128)S(1)} all-reduce(f32[2,1,1,1]{0,3,2,1:T(1,128)S(1)} %bitcast.94), channel_id=1, replica_groups=mesh['sec'=32,'blk'=16] {'blk'}, use_global_device_ids=true, to_apply=%region_16.17 | all-reduce | flops 2 | bytes 16 | tf_op jit(solution)/shard_map/psum | solution.py:115
  338.2 1.3 collective-permute-start.7
  339.5 3.0 collective-permute-start.8
  342.6 0.8 collective-permute-done.8
  343.4 0.3 fusion.26
  343.7 47.7 %psum.63 = f32[2,1,1,1]{0,3,2,1:T(1,128)S(1)} all-reduce(f32[2,1,1,1]{0,3,2,1:T(1,128)S(1)} %bitcast.91), channel_id=1, replica_groups=mesh['sec'=32,'blk'=16] {'blk'}, use_global_device_ids=true, to_apply=%region_18.19 | all-reduce | flops 2 | bytes 16 | tf_op jit(solution)/shard_map/psum | solution.py:123
  391.4 0.8 multiply_add_fusion
  (34 shorter events, 1.2 us)
Async XLA Ops:
  3.7 30.7 %collective-permute-start = (bf16[1,128,4096]{1,2,0:T(8,128)(2,1)S(1)}, bf16[1,128,4096]{1,2,0:T(8,128)(2,1)S(1)}, u32[]{:S(2)}, u32[]{:S(2)}) collective-permute-start(bf16[1,128,4096]{1,2,0:T(8,128)(2,1)S(1)} %convert_multiply_fusion.4), channel_id=1, source_target_pairs={{16,0},{32,16},{48,32},{64,48},{80,64},{96,80},{112,96},{128,112},... | collective-permute-start | bytes 3145736 | tf_op jit(solution)/shard_map/ppermute | solution.py:35
  6.7 1.3 copy-start
  7.4 0.9 copy-start.3
  43.8 3.9 %copy-start.1 = (f32[32,1024]{1,0:T(8,128)S(1)}, f32[32,1024]{1,0:T(8,128)}, u32[]{:S(2)}) copy-start(f32[32,1024]{1,0:T(8,128)} %get-tuple-element.40) | copy-start | bytes 393220
  43.8 4.0 %copy-start.2 = (f32[2,1,32,1024]{3,2,1,0:T(8,128)S(1)}, f32[2,1,32,1024]{3,2,1,0:T(8,128)}, u32[]{:S(2)}) copy-start(f32[2,1,32,1024]{3,2,1,0:T(8,128)} %param.9) | copy-start | bytes 786436
  47.8 4.5 %collective-permute-start.1 = (bf16[2,1,1,1024]{3,2,1,0:T(2,128)(2,1)S(1)}, bf16[2,1,1,1024]{3,2,1,0:T(2,128)(2,1)S(1)}, u32[]{:S(2)}, u32[]{:S(2)}) collective-permute-start(bf16[2,1,1,1024]{3,2,1,0:T(2,128)(2,1)S(1)} %get-tuple-element.41), channel_id=1, source_target_pairs={{1,0},{2,1},{3,2},{4,3},{5,4},{6,5},{7,6},{8,7},{9,8},{10,9},{11,1... | collective-permute-start | bytes 12296 | tf_op jit(solution)/shard_map/ppermute | solution.py:27
  49.3 3.8 collective-permute-start.2
  145.6 4.3 %collective-permute-start.3 = (bf16[2,1,1,1024]{3,2,1,0:T(2,128)(2,1)S(1)}, bf16[2,1,1,1024]{3,2,1,0:T(2,128)(2,1)S(1)}, u32[]{:S(2)}, u32[]{:S(2)}) collective-permute-start(bf16[2,1,1,1024]{3,2,1,0:T(2,128)(2,1)S(1)} %get-tuple-element.37), channel_id=1, source_target_pairs={{1,0},{2,1},{3,2},{4,3},{5,4},{6,5},{7,6},{8,7},{9,8},{10,9},{11,1... | collective-permute-start | bytes 12296 | tf_op jit(solution)/shard_map/ppermute | solution.py:27
  146.9 3.8 collective-permute-start.4
  241.9 4.3 %collective-permute-start.5 = (bf16[2,1,1,1024]{3,2,1,0:T(2,128)(2,1)S(1)}, bf16[2,1,1,1024]{3,2,1,0:T(2,128)(2,1)S(1)}, u32[]{:S(2)}, u32[]{:S(2)}) collective-permute-start(bf16[2,1,1,1024]{3,2,1,0:T(2,128)(2,1)S(1)} %get-tuple-element.35), channel_id=1, source_target_pairs={{1,0},{2,1},{3,2},{4,3},{5,4},{6,5},{7,6},{8,7},{9,8},{10,9},{11,1... | collective-permute-start | bytes 12296 | tf_op jit(solution)/shard_map/ppermute | solution.py:27
  243.2 3.8 collective-permute-start.6
  338.2 4.3 %collective-permute-start.7 = (bf16[2,1,1,1024]{3,2,1,0:T(2,128)(2,1)S(1)}, bf16[2,1,1,1024]{3,2,1,0:T(2,128)(2,1)S(1)}, u32[]{:S(2)}, u32[]{:S(2)}) collective-permute-start(bf16[2,1,1,1024]{3,2,1,0:T(2,128)(2,1)S(1)} %get-tuple-element.33), channel_id=1, source_target_pairs={{1,0},{2,1},{3,2},{4,3},{5,4},{6,5},{7,6},{8,7},{9,8},{10,9},{11,1... | collective-permute-start | bytes 12296 | tf_op jit(solution)/shard_map/ppermute | solution.py:27
  339.5 3.8 collective-permute-start.8
where the time goes:
time: 393 us; the launch traced here: 392 us
  blocking collectives  320 us (81%)
  waiting for transfers between devices  26.6 us (7%)
  starting transfers between devices  19.8 us (5%)
  matrix products  17 us (4%)
  other arithmetic  4.15 us (1%)
  local copies, waits for them, and re-layouts  3.98 us (1%)
    psum x4, blocking collectives, squares(): return lax.psum(section_dot(residual, residual), 'blk')  177 us
    psum x3, blocking collectives, per_device(): alpha = norm_now / lax.psum(section_dot(direction, image_dir), 'blk')  143 us
    ppermute x1, waiting for transfers between devices, shifted(): lax.ppermute(value, axis, [(source, source + steps) for source in range(l...  23.4 us
    ppermute x4, starting transfers between devices, extended(): lax.ppermute(lax.slice_in_dim(block, block.shape[dim] - width, None, axis...  12.1 us
    dot_general x10, matrix products, along_cols(): jnp.einsum('kpj,jl->kpl', block, table, preferred_element_type=jnp.float32)  11.9 us
  transfers between devices with their start and end apart: 9, of which 5 were waited for; matrix products, arithmetic and copies ran while one was open for 1% of the time, Pallas kernels for 0%

commit v1 on v0

v1 whole, which is shorter than its diff:
```python
import functools
import math

import jax
import jax.numpy as jnp
import ml_dtypes
import numpy as np
from jax import lax
from jax.experimental import pallas as pl
from jax.experimental.pallas import tpu as pltpu
from jax.sharding import PartitionSpec as P

MESH = pl.DeviceIdType.MESH
ITERS = 4
SIZE = 128
PAIR = 2 * SIZE
LANES = 128
EDGE = 8
SPAN = 4
SHIFTS = (1.0, 4.0, 1.0, 4.0)
SCALE = 0.25
PAIRS = tuple((i, j) for i in range(ITERS) for j in range(i, ITERS)) + tuple((i, ITERS) for i in range(ITERS))


def tables():
    j = np.arange(SIZE)
    angle = (j[:, None] * j[None, :] % SIZE).astype(np.float32) * np.float32(2.0 * math.pi / SIZE)
    cosine = np.cos(angle).astype(ml_dtypes.bfloat16)
    sine = np.sin(angle).astype(ml_dtypes.bfloat16)
    both = np.block([[cosine, -sine], [sine, cosine]])
    return both, np.concatenate([cosine, -sine], axis=0)


def matmul(left, right):
    return jnp.dot(left, right, preferred_element_type=jnp.float32)


def beside(pair):
    rows = [
        jnp.concatenate([pair[:SIZE, p * SIZE : (p + 1) * SIZE], pair[SIZE:, p * SIZE : (p + 1) * SIZE]], axis=1)
        for p in range(2)
    ]
    return jnp.concatenate(rows, axis=0)


def stacked(re, im):
    rows = [jnp.concatenate([part[:SIZE], part[SIZE:]], axis=1) for part in (re, im)]
    return jnp.concatenate(rows, axis=0)


def spectrum(block, narrow, both):
    half = matmul(narrow, block).astype(jnp.bfloat16)
    return matmul(beside(half), both).astype(jnp.bfloat16)


def offsets(shape, axis):
    index = lax.broadcasted_iota(jnp.int32, shape, axis)
    return (((index + SIZE // 2) % SIZE) - SIZE // 2).astype(jnp.float32)


def flows_of(own, other, narrow, both):
    a = own.astype(jnp.float32)
    b = other.astype(jnp.float32)
    a_re, a_im, b_re, b_im = a[:, :SIZE], a[:, SIZE:], b[:, :SIZE], b[:, SIZE:]
    cross_re = (a_re * b_re + a_im * b_im).astype(jnp.bfloat16)
    cross_im = (a_im * b_re - a_re * b_im).astype(jnp.bfloat16)
    back = matmul(both, stacked(cross_re, cross_im)).astype(jnp.bfloat16)
    corr = matmul(beside(back), narrow)
    weight = (corr * corr).reshape(2, SIZE, SIZE)
    whole = jnp.sum(weight, axis=1)
    tilted = jnp.sum(weight * offsets((1, SIZE, SIZE), 1), axis=1)
    unit = 2.0**-42
    total = jnp.sum(whole, axis=1, keepdims=True) * unit + 1e-6
    row_flow = jnp.sum(tilted, axis=1, keepdims=True) * unit / total
    col_flow = jnp.sum(whole * offsets((2, SIZE), 1), axis=1, keepdims=True) * unit / total
    return row_flow, col_flow


def neighbours(value):
    tiles, rows, _ = value.shape
    lane = lax.broadcasted_iota(jnp.int32, value.shape, 2)
    none = jnp.zeros((1, rows, LANES), value.dtype)
    right = pltpu.roll(value, 1, 2)
    right = jnp.where(lane == 0, jnp.concatenate([none, right[:-1]], axis=0), right)
    left = pltpu.roll(value, LANES - 1, 2)
    left = jnp.where(lane == LANES - 1, jnp.concatenate([left[1:], none], axis=0), left)
    return pltpu.roll(value, 1, 1) + pltpu.roll(value, rows - 1, 1) + right + left


def coefficients(gram):
    def inner(left, right):
        terms = [l * r * gram[min(i, j), max(i, j)] for i, l in enumerate(left) for j, r in enumerate(right)]
        return functools.reduce(lambda p, q: p + q, terms)

    zero = jnp.zeros_like(gram[0, 0])
    solution = [zero] * ITERS
    residual = [jnp.ones_like(zero)]
    direction = list(residual)
    norm_now = gram[0, 0]
    for step in range(ITERS):
        image = [SHIFTS[j] * direction[j] for j in range(step + 1)] + [zero]
        image = [image[j] + (direction[j - 1] / SCALE if j else 0.0) for j in range(step + 2)]
        curve = inner(direction, image)
        alpha = jnp.where(curve > 0.0, jnp.clip(norm_now / curve, 0.0, 10.1), 0.0)
        solution = [solution[j] + alpha * direction[j] if j <= step else solution[j] for j in range(ITERS)]
        if step == ITERS - 1:
            break
        residual = [r - alpha * i for r, i in zip(residual + [zero], image)]
        norm_next = jnp.maximum(inner(residual, residual), 0.0)
        beta = jnp.where(norm_now > 0.0, norm_next / norm_now, 0.0)
        direction = [r + beta * d for r, d in zip(residual, direction + [zero])]
        norm_now = norm_next
    return solution


def kernel(
    sections,
    bands,
    image_hbm,
    mask_hbm,
    anchor_hbm,
    fixed_hbm,
    prior_hbm,
    both_hbm,
    narrow_hbm,
    out_ref,
    image,
    mask,
    masked,
    arrived,
    spectra,
    both,
    narrow,
    anchor,
    fixed,
    prior,
    edge_out,
    edge_in,
    pull,
    diag,
    link,
    base,
    flow,
    flow_in,
    basis,
    share,
    shares,
    load_sem,
    mesh_sem,
    send_sem,
    recv_sem,
    edge_send,
    edge_recv,
    flow_send,
    flow_recv,
    share_send,
    share_recv,
):
    chunks = image.shape[0]
    tiles = pull.shape[0]
    rows = anchor.shape[0]
    sec = lax.axis_index("sec")
    blk = lax.axis_index("blk")
    has_above, has_below = blk > 0, blk < bands - 1
    has_prev, has_next = sec > 0, sec < sections - 1
    others = [lax.rem(blk + d, bands) for d in range(1, bands)]

    def pixels(c):
        return pl.ds(pl.multiple_of(c * PAIR, PAIR), PAIR)

    def loads(c):
        return (
            pltpu.make_async_copy(image_hbm.at[0, :, pixels(c)], image.at[c], load_sem.at[0, c]),
            pltpu.make_async_copy(mask_hbm.at[0, :, pixels(c)], mask.at[c], load_sem.at[1, c]),
        )

    def sent(c):
        return pltpu.make_async_remote_copy(
            masked.at[c], arrived.at[c], send_sem.at[c], recv_sem.at[c], device_id={"sec": sec - 1}, device_id_type=MESH
        )

    mesh_loads = [
        pltpu.make_async_copy(both_hbm, both, mesh_sem.at[0]),
        pltpu.make_async_copy(narrow_hbm, narrow, mesh_sem.at[1]),
        pltpu.make_async_copy(anchor_hbm.at[0], anchor, mesh_sem.at[2]),
        pltpu.make_async_copy(fixed_hbm.at[0], fixed, mesh_sem.at[3]),
        pltpu.make_async_copy(prior_hbm.at[:, 0], prior, mesh_sem.at[4]),
    ]

    barrier = pltpu.get_barrier_semaphore()

    def greet(device):
        pl.semaphore_signal(barrier, inc=1, device_id=device, device_id_type=MESH)

    pl.when(has_prev)(lambda: greet({"sec": sec - 1}))
    pl.when(has_next)(lambda: greet({"sec": sec + 1}))
    for other in others:
        greet({"blk": other})

    def start_loads(c, _):
        for copy in loads(c):
            copy.start()
        return 0

    lax.fori_loop(0, 4, start_loads, 0)
    for copy in mesh_loads:
        copy.start()
    lax.fori_loop(4, chunks, start_loads, 0)

    def hide(c):
        for copy in loads(c):
            copy.wait()
        masked[c] = image[c] * mask[c].astype(jnp.float32).astype(jnp.bfloat16)

    def hide_and_send(c, _):
        hide(c)
        pl.when(has_prev)(lambda: sent(c).start())
        return 0

    hide(0)
    pl.semaphore_wait(barrier, bands - 1 + has_prev.astype(jnp.int32) + has_next.astype(jnp.int32))
    pl.when(has_prev)(lambda: sent(0).start())
    lax.fori_loop(1, 4, hide_and_send, 0)

    for copy in mesh_loads:
        copy.wait()
    free = 1.0 - fixed[...].astype(jnp.float32)
    own_pull = free * anchor[...]
    own = [own_pull, own_pull * prior[0], own_pull * prior[1]]

    def edge_copy(up):
        slot = 0 if up else 1
        return pltpu.make_async_remote_copy(
            edge_out.at[slot],
            edge_in.at[slot],
            edge_send.at[slot],
            edge_recv.at[slot],
            device_id={"blk": blk - 1 if up else blk + 1},
            device_id_type=MESH,
        )

    def flow_copy(up):
        slot = 0 if up else 1
        return pltpu.make_async_remote_copy(
            flow,
            flow_in.at[slot],
            flow_send.at[slot],
            flow_recv.at[slot],
            device_id={"blk": blk - 1 if up else blk + 1},
            device_id_type=MESH,
        )

    width = 3 * tiles * LANES // 4

    def packed(first):
        flat = jnp.concatenate([part[first : first + SPAN] for part in own], axis=1)
        return jnp.concatenate([flat[:, k * width : (k + 1) * width] for k in range(4)], axis=0).astype(jnp.bfloat16)

    def unpacked(block):
        block = block.astype(jnp.float32)
        flat = jnp.concatenate([block[k * SPAN : (k + 1) * SPAN] for k in range(4)], axis=1)
        return [flat[:, k * tiles * LANES : (k + 1) * tiles * LANES] for k in range(3)]

    edge_out[0] = packed(0)
    edge_out[1] = packed(rows - SPAN)
    pl.when(has_above)(lambda: edge_copy(True).start())
    pl.when(has_below)(lambda: edge_copy(False).start())
    lax.fori_loop(4, chunks, hide_and_send, 0)

    def own_spectrum(c, _):
        spectra[c] = spectrum(masked[c], narrow[...], both[...])
        return 0

    lax.fori_loop(0, chunks, own_spectrum, 0)

    pull[...] = jnp.zeros_like(pull)
    base[...] = jnp.zeros_like(base)
    for g in range(tiles):
        at = slice(g * LANES, (g + 1) * LANES)
        pull[g, EDGE : EDGE + rows] = own[0][:, at]
        base[0, g, EDGE : EDGE + rows] = own[1][:, at]
        base[1, g, EDGE : EDGE + rows] = own[2][:, at]

    def take_edge(slot, first):
        parts = unpacked(edge_in[slot])
        for g in range(tiles):
            at = slice(g * LANES, (g + 1) * LANES)
            pull[g, first : first + SPAN] = parts[0][:, at]
            base[0, g, first : first + SPAN] = parts[1][:, at]
            base[1, g, first : first + SPAN] = parts[2][:, at]

    @pl.when(has_below)
    def _():
        edge_copy(True).wait_recv()
        take_edge(0, EDGE + rows)

    @pl.when(has_above)
    def _():
        edge_copy(False).wait_recv()
        take_edge(1, EDGE - SPAN)

    loose = jnp.where(pull[...] > 0.0, SCALE, 0.0)
    link[...] = loose
    diag[...] = 4.0 * loose + SCALE * pull[...]

    flow[...] = jnp.zeros_like(flow)
    tile_row = lax.broadcasted_iota(jnp.int32, (tiles, LANES), 0)
    quarter = lax.broadcasted_iota(jnp.int32, (tiles, LANES), 1) // (LANES // 4)

    def correlate(c, _):
        sent(c).wait_recv()
        other = spectrum(arrived[c], narrow[...], both[...])
        for k, value in enumerate(flows_of(spectra[c], other, narrow[...], both[...])):
            held = flow[k]
            for p in range(2):
                here = (tile_row == c // 2) & (quarter == 2 * (c % 2) + p)
                held = jnp.where(here, value[p : p + 1], held)
            flow[k] = held
        return 0

    @pl.when(has_next)
    def _():
        lax.fori_loop(0, chunks, correlate, 0)

    pl.when(has_above)(lambda: flow_copy(True).start())
    pl.when(has_below)(lambda: flow_copy(False).start())

    @pl.when(has_below)
    def _():
        flow_copy(True).wait_recv()

    @pl.when(has_above)
    def _():
        flow_copy(False).wait_recv()

    @pl.when(jnp.logical_not(has_below))
    def _():
        flow_in[0] = jnp.zeros_like(flow)

    @pl.when(jnp.logical_not(has_above))
    def _():
        flow_in[1] = jnp.zeros_like(flow)

    for k in range(2):
        for g in range(tiles):
            for source, first, count in (
                (flow_in.at[1], 0, EDGE),
                (flow, EDGE, rows),
                (flow_in.at[0], EDGE + rows, EDGE),
            ):
                at = slice(first, first + count)
                basis[k, 0, g, at] = base[k, g, at] + pull[g, at] * source[k, g : g + 1, :]

    lane = lax.broadcasted_iota(jnp.int32, (8, LANES), 1)
    sums = []
    for k in range(2):
        for step in range(ITERS):
            value = basis[k, step]
            basis[k, step + 1] = (diag[...] - SCALE * SHIFTS[step]) * value - link[...] * neighbours(value)
        lines = []
        for i, j in PAIRS:
            product = basis[k, i, :, EDGE : EDGE + rows] * basis[k, j, :, EDGE : EDGE + rows]
            total = jnp.sum(product.reshape(tiles * rows // 8, 8, LANES), axis=0)
            lines.append(jnp.sum(total, axis=0, keepdims=True))
        lines += [jnp.zeros((1, LANES), jnp.float32)] * (16 - len(lines))
        for half in range(2):
            block = jnp.concatenate(lines[8 * half : 8 * half + 8], axis=0)
            block = block + pltpu.roll(block, LANES // 2, 1)
            sums.append(block + pltpu.roll(block, LANES // 4, 1))
    part = lane // (LANES // 4)
    mine = sums[3]
    for n in range(3):
        mine = jnp.where(part == n, sums[n], mine)
    share[...] = mine

    def share_copy(n):
        return pltpu.make_async_remote_copy(
            share,
            shares.at[blk],
            share_send.at[n],
            share_recv.at[n],
            device_id={"blk": others[n]},
            device_id_type=MESH,
        )

    for n in range(bands - 1):
        share_copy(n).start()
    shares[blk] = share[...]
    for n in range(bands - 1):
        share_copy(n).wait_recv()
    total = jnp.sum(shares[...], axis=0)
    quarters = [jnp.sum(jnp.where(part == n, total, 0.0), axis=1, keepdims=True) for n in range(4)]
    gram = {}
    for n, pair in enumerate(PAIRS):
        line = [quarters[2 * k + n // 8][n % 8 : n % 8 + 1] for k in range(2)]
        gram[pair] = jnp.where(lane[:1] < LANES // 2, line[0], line[1])
    found = coefficients(gram)
    for k in range(2):
        weights = [value[:, k * LANES // 2 : k * LANES // 2 + 1] for value in found]
        for g in range(tiles):
            at = slice(EDGE, EDGE + rows)
            value = weights[0] * basis[k, 0, g, at]
            for step in range(1, ITERS):
                value = value + weights[step] * basis[k, step, g, at]
            out_ref[k, :, g * LANES : (g + 1) * LANES] = value

    for n in range(bands - 1):
        share_copy(n).wait_send()

    @pl.when(has_above)
    def _():
        edge_copy(True).wait_send()
        flow_copy(True).wait_send()

    @pl.when(has_below)
    def _():
        edge_copy(False).wait_send()
        flow_copy(False).wait_send()

    def drain(c, _):
        sent(c).wait_send()
        return 0

    @pl.when(has_prev)
    def _():
        lax.fori_loop(0, chunks, drain, 0)


def per_device(sections, bands, image, tissue_mask, anchor, fixed_nodes, prior_shift):
    _, size, columns = image.shape
    _, rows, nodes = anchor.shape
    chunks = columns // PAIR
    tiles = nodes // LANES
    wide = 2 * EDGE + rows
    width = 3 * nodes // 4
    both, narrow = tables()
    out = pl.pallas_call(
        functools.partial(kernel, sections, bands),
        out_shape=jax.ShapeDtypeStruct((2, rows, nodes), jnp.float32),
        in_specs=[pl.BlockSpec(memory_space=pl.ANY)] * 7,
        out_specs=pl.BlockSpec(memory_space=pltpu.VMEM),
        scratch_shapes=[
            pltpu.VMEM((chunks, size, PAIR), jnp.bfloat16),
            pltpu.VMEM((chunks, size, PAIR), jnp.int32),
            pltpu.VMEM((chunks, size, PAIR), jnp.bfloat16),
            pltpu.VMEM((chunks, size, PAIR), jnp.bfloat16),
            pltpu.VMEM((chunks, PAIR, PAIR), jnp.bfloat16),
            pltpu.VMEM((PAIR, PAIR), jnp.bfloat16),
            pltpu.VMEM((PAIR, SIZE), jnp.bfloat16),
            pltpu.VMEM((rows, nodes), jnp.float32),
            pltpu.VMEM((rows, nodes), jnp.int32),
            pltpu.VMEM((2, rows, nodes), jnp.float32),
            pltpu.VMEM((2, 4 * SPAN, width), jnp.bfloat16),
            pltpu.VMEM((2, 4 * SPAN, width), jnp.bfloat16),
            pltpu.VMEM((tiles, wide, LANES), jnp.float32),
            pltpu.VMEM((tiles, wide, LANES), jnp.float32),
            pltpu.VMEM((tiles, wide, LANES), jnp.float32),
            pltpu.VMEM((2, tiles, wide, LANES), jnp.float32),
            pltpu.VMEM((2, tiles, LANES), jnp.float32),
            pltpu.VMEM((2, 2, tiles, LANES), jnp.float32),
            pltpu.VMEM((2, ITERS + 1, tiles, wide, LANES), jnp.float32),
            pltpu.VMEM((8, LANES), jnp.float32),
            pltpu.VMEM((bands, 8, LANES), jnp.float32),
            pltpu.SemaphoreType.DMA((2, chunks)),
            pltpu.SemaphoreType.DMA((5,)),
            pltpu.SemaphoreType.DMA((chunks,)),
            pltpu.SemaphoreType.DMA((chunks,)),
            pltpu.SemaphoreType.DMA((2,)),
            pltpu.SemaphoreType.DMA((2,)),
            pltpu.SemaphoreType.DMA((2,)),
            pltpu.SemaphoreType.DMA((2,)),
            pltpu.SemaphoreType.DMA((bands - 1,)),
            pltpu.SemaphoreType.DMA((bands - 1,)),
        ],
        compiler_params=pltpu.CompilerParams(
            collective_id=0, has_side_effects=True, vmem_limit_bytes=40 * 1024 * 1024
        ),
        cost_estimate=pl.CostEstimate(flops=2_400_000_000, bytes_accessed=4_000_000, transcendentals=0),
    )(image, tissue_mask, anchor, fixed_nodes, prior_shift, jnp.asarray(both), jnp.asarray(narrow))
    return out[:, None]


def solution(mesh):
    sections, bands = mesh.shape["sec"], mesh.shape["blk"]
    return jax.shard_map(
        functools.partial(per_device, sections, bands),
        mesh=mesh,
        in_specs=(
            P("sec", "blk", None),
            P("sec", "blk", None),
            P("sec", "blk", None),
            P("sec", "blk", None),
            P(None, "sec", "blk", None),
        ),
        out_specs=P(None, "sec", "blk", None),
        check_vma=False,
    )
```

time: 393 us -> 66.7 us (0.17)
  the two profiles are of different devices: /device:TPU:216 before, /device:TPU:337 now
where the time goes in v1:
time: 66.7 us; the launch traced here: 66.4 us
  Pallas kernels  58.3 us (87%)
  local copies, waits for them, and re-layouts  8.02 us (12%)
    pallas_call x1, Pallas kernels, per_device(): pl.pallas_call(functools.partial(kernel, sections, bands), out_shape=jax....  58.3 us
    unnamed x15, local copies, waits for them, and re-layouts  8.02 us

profile of v1, /device:TPU:337, one launch (start us, length us, event | category | flops | bytes accessed | tf_op | source)
XLA Modules:
  0.0 66.4 jit_solution(11286964640368622290)
XLA Ops:
  0.0 0.0 copy-start
  0.0 1.6 %copy-done = s32[1,128,4096]{2,1,0:T(8,128)S(1)} copy-done((s32[1,128,4096]{2,1,0:T(8,128)S(1)}, s32[1,128,4096]{2,1,0:T(8,128)}, u32[]{:S(2)}) %copy-start) | copy-done | bytes 2097176
  1.6 0.0 copy-start.1
  1.6 1.2 %copy-done.1 = bf16[1,128,4096]{2,1,0:T(8,128)(2,1)S(1)} copy-done((bf16[1,128,4096]{2,1,0:T(8,128)(2,1)S(1)}, bf16[1,128,4096]{2,1,0:T(8,128)(2,1)}, u32[]{:S(2)}) %copy-start.1) | copy-done | bytes 1048600
  2.8 0.0 copy-start.2
  2.8 0.9 %copy-done.2 = f32[2,1,32,1024]{3,2,1,0:T(8,128)S(1)} copy-done((f32[2,1,32,1024]{3,2,1,0:T(8,128)S(1)}, f32[2,1,32,1024]{3,2,1,0:T(8,128)}, u32[]{:S(2)}) %copy-start.2) | copy-done | bytes 262168
  3.8 0.0 copy-start.3
  3.8 0.9 %copy-done.3 = f32[1,32,1024]{2,1,0:T(8,128)S(1)} copy-done((f32[1,32,1024]{2,1,0:T(8,128)S(1)}, f32[1,32,1024]{2,1,0:T(8,128)}, u32[]{:S(2)}) %copy-start.3) | copy-done | bytes 131096
  4.7 0.0 copy-start.4
  4.7 0.9 %copy-done.4 = s32[1,32,1024]{2,1,0:T(8,128)S(1)} copy-done((s32[1,32,1024]{2,1,0:T(8,128)S(1)}, s32[1,32,1024]{2,1,0:T(8,128)}, u32[]{:S(2)}) %copy-start.4) | copy-done | bytes 131096
  5.6 0.0 copy-start.5
  5.6 0.9 %copy-done.5 = bf16[256,256]{1,0:T(8,128)(2,1)S(1)} copy-done((bf16[256,256]{1,0:T(8,128)(2,1)S(1)}, bf16[256,256]{1,0:T(8,128)(2,1)}, u32[]{:S(2)}) %copy-start.5) | copy-done | bytes 131096
  6.5 0.0 copy-start.6
  6.5 0.8 %copy-done.6 = bf16[256,128]{1,0:T(8,128)(2,1)S(1)} copy-done((bf16[256,128]{1,0:T(8,128)(2,1)S(1)}, bf16[256,128]{1,0:T(8,128)(2,1)}, u32[]{:S(2)}) %copy-start.6) | copy-done | bytes 65560
  7.3 58.3 %shard_map.73 = f32[2,32,1024]{2,1,0:T(8,128)S(1)} custom-call(bf16[1,128,4096]{2,1,0:T(8,128)(2,1)S(1)} %copy-done.1, s32[1,128,4096]{2,1,0:T(8,128)S(1)} %copy-done, f32[1,32,1024]{2,1,0:T(8,128)S(1)} %copy-done.3, s32[1,32,1024]{2,1,0:T(8,128)S(1)} %copy-done.4, f32[2,1,32,1024]{3,2,1,0:T(8,128)S(1)} %copy-done.2, bf16[256,256]{1,0:T(8,128)(2,1)S(1)} %copy-done.5, ...), custom_call_target="tpu_custom_call" | custom-call | flops 2400000000 | bytes 4000000 | tf_op jit(solution)/shard_map/pallas_call | solution.py:437
  65.7 0.7 %copy.10 = f32[2,1,32,1024]{3,2,1,0:T(8,128)} copy(f32[2,1,32,1024]{3,2,1,0:T(8,128)S(1)} %bitcast.3) | data formatting | bytes 524288
Async XLA Ops:
  0.0 1.6 %copy-start = (s32[1,128,4096]{2,1,0:T(8,128)S(1)}, s32[1,128,4096]{2,1,0:T(8,128)}, u32[]{:S(2)}) copy-start(s32[1,128,4096]{2,1,0:T(8,128)} %mask_hbm.1) | copy-start | bytes 6291460
  1.6 1.2 %copy-start.1 = (bf16[1,128,4096]{2,1,0:T(8,128)(2,1)S(1)}, bf16[1,128,4096]{2,1,0:T(8,128)(2,1)}, u32[]{:S(2)}) copy-start(bf16[1,128,4096]{2,1,0:T(8,128)(2,1)} %image_hbm.1) | copy-start | bytes 3145732
  2.8 0.9 %copy-start.2 = (f32[2,1,32,1024]{3,2,1,0:T(8,128)S(1)}, f32[2,1,32,1024]{3,2,1,0:T(8,128)}, u32[]{:S(2)}) copy-start(f32[2,1,32,1024]{3,2,1,0:T(8,128)} %prior_hbm.1) | copy-start | bytes 786436
  3.8 0.9 %copy-start.3 = (f32[1,32,1024]{2,1,0:T(8,128)S(1)}, f32[1,32,1024]{2,1,0:T(8,128)}, u32[]{:S(2)}) copy-start(f32[1,32,1024]{2,1,0:T(8,128)} %anchor_hbm.1) | copy-start | bytes 393220
  4.7 0.9 %copy-start.4 = (s32[1,32,1024]{2,1,0:T(8,128)S(1)}, s32[1,32,1024]{2,1,0:T(8,128)}, u32[]{:S(2)}) copy-start(s32[1,32,1024]{2,1,0:T(8,128)} %fixed_hbm.1) | copy-start | bytes 393220
  5.6 0.9 %copy-start.5 = (bf16[256,256]{1,0:T(8,128)(2,1)S(1)}, bf16[256,256]{1,0:T(8,128)(2,1)}, u32[]{:S(2)}) copy-start(bf16[256,256]{1,0:T(8,128)(2,1)} %constant.4.clone.both_hbm) | copy-start | bytes 393220
  6.5 0.8 %copy-start.6 = (bf16[256,128]{1,0:T(8,128)(2,1)S(1)}, bf16[256,128]{1,0:T(8,128)(2,1)}, u32[]{:S(2)}) copy-start(bf16[256,128]{1,0:T(8,128)(2,1)} %constant.5.clone.narrow_hbm) | copy-start | bytes 196612

commit v2 on v1

--- a/solution.py
+++ b/solution.py
@@ -155,6 +155,7 @@
     flow_recv,
     share_send,
     share_recv,
+    round_sem,
 ):
     chunks = image.shape[0]
     tiles = pull.shape[0]
@@ -163,7 +164,18 @@
     blk = lax.axis_index("blk")
     has_above, has_below = blk > 0, blk < bands - 1
     has_prev, has_next = sec > 0, sec < sections - 1
-    others = [lax.rem(blk + d, bands) for d in range(1, bands)]
+    turns = bands // 4
+    here = (blk // 4, lax.rem(blk // 2, 2), lax.rem(blk, 2))
+
+    def moved(dx, dy, dc):
+        return lax.rem(here[0] + dx, turns) * 4 + lax.rem(here[1] + dy, 2) * 2 + lax.rem(here[2] + dc, 2)
+
+    order = [dx if dx <= turns // 2 else dx - turns for dx in range(turns)]
+    steps = sorted(
+        ((dx % turns, dy, dc) for dx in order for dy in range(2) for dc in range(2)),
+        key=lambda step: (-step[1], -min(step[0], turns - step[0]), -step[2]),
+    )
+    others = [moved(*step) for step in steps if any(step)]
 
     def pixels(c):
         return pl.ds(pl.multiple_of(c * PAIR, PAIR), PAIR)
@@ -194,7 +206,11 @@
 
     pl.when(has_prev)(lambda: greet({"sec": sec - 1}))
     pl.when(has_next)(lambda: greet({"sec": sec + 1}))
-    for other in others:
+    pl.when(has_above)(lambda: greet({"blk": blk - 1}))
+    pl.when(has_below)(lambda: greet({"blk": blk + 1}))
+    across, over = moved(0, 0, 1), moved(0, 1, 0)
+    along = [moved(dx, 0, 0) for dx in range(1, turns)]
+    for other in [across, over] + along:
         greet({"blk": other})
 
     def start_loads(c, _):
@@ -202,10 +218,10 @@
             copy.start()
         return 0
 
-    lax.fori_loop(0, 4, start_loads, 0)
+    lax.fori_loop(0, 1, start_loads, 0)
     for copy in mesh_loads:
         copy.start()
-    lax.fori_loop(4, chunks, start_loads, 0)
+    lax.fori_loop(1, chunks, start_loads, 0)
 
     def hide(c):
         for copy in loads(c):
@@ -218,10 +234,6 @@
         return 0
 
     hide(0)
-    pl.semaphore_wait(barrier, bands - 1 + has_prev.astype(jnp.int32) + has_next.astype(jnp.int32))
-    pl.when(has_prev)(lambda: sent(0).start())
-    lax.fori_loop(1, 4, hide_and_send, 0)
-
     for copy in mesh_loads:
         copy.wait()
     free = 1.0 - fixed[...].astype(jnp.float32)
@@ -263,15 +275,23 @@
 
     edge_out[0] = packed(0)
     edge_out[1] = packed(rows - SPAN)
+    greeted = has_prev, has_next, has_above, has_below
+    pl.semaphore_wait(barrier, turns + 1 + functools.reduce(lambda p, q: p + q, [g.astype(jnp.int32) for g in greeted]))
     pl.when(has_above)(lambda: edge_copy(True).start())
     pl.when(has_below)(lambda: edge_copy(False).start())
-    lax.fori_loop(4, chunks, hide_and_send, 0)
+    pl.when(has_prev)(lambda: sent(0).start())
+    pl.semaphore_signal(round_sem.at[0], inc=1, device_id={"blk": across}, device_id_type=MESH)
+    lax.fori_loop(1, 8, hide_and_send, 0)
+    pl.semaphore_wait(round_sem.at[0], 1)
+    pl.semaphore_signal(round_sem.at[1], inc=1, device_id={"blk": over}, device_id_type=MESH)
+    lax.fori_loop(8, chunks, hide_and_send, 0)
 
     def own_spectrum(c, _):
         spectra[c] = spectrum(masked[c], narrow[...], both[...])
         return 0
 
     lax.fori_loop(0, chunks, own_spectrum, 0)
+    pl.semaphore_wait(round_sem.at[1], 1)
 
     pull[...] = jnp.zeros_like(pull)
     base[...] = jnp.zeros_like(base)
@@ -289,20 +309,6 @@
             base[0, g, first : first + SPAN] = parts[1][:, at]
             base[1, g, first : first + SPAN] = parts[2][:, at]
 
-    @pl.when(has_below)
-    def _():
-        edge_copy(True).wait_recv()
-        take_edge(0, EDGE + rows)
-
-    @pl.when(has_above)
-    def _():
-        edge_copy(False).wait_recv()
-        take_edge(1, EDGE - SPAN)
-
-    loose = jnp.where(pull[...] > 0.0, SCALE, 0.0)
-    link[...] = loose
-    diag[...] = 4.0 * loose + SCALE * pull[...]
-
     flow[...] = jnp.zeros_like(flow)
     tile_row = lax.broadcasted_iota(jnp.int32, (tiles, LANES), 0)
     quarter = lax.broadcasted_iota(jnp.int32, (tiles, LANES), 1) // (LANES // 4)
@@ -313,14 +319,34 @@
         for k, value in enumerate(flows_of(spectra[c], other, narrow[...], both[...])):
             held = flow[k]
             for p in range(2):
-                here = (tile_row == c // 2) & (quarter == 2 * (c % 2) + p)
-                held = jnp.where(here, value[p : p + 1], held)
+                spot = (tile_row == c // 2) & (quarter == 2 * (c % 2) + p)
+                held = jnp.where(spot, value[p : p + 1], held)
             flow[k] = held
         return 0
 
+    late = chunks * 3 // 4
+
     @pl.when(has_next)
     def _():
-        lax.fori_loop(0, chunks, correlate, 0)
+        lax.fori_loop(0, late, correlate, 0)
+
+    @pl.when(has_below)
+    def _():
+        edge_copy(True).wait_recv()
+        take_edge(0, EDGE + rows)
+
+    @pl.when(has_above)
+    def _():
+        edge_copy(False).wait_recv()
+        take_edge(1, EDGE - SPAN)
+
+    loose = jnp.where(pull[...] > 0.0, SCALE, 0.0)
+    link[...] = loose
+    diag[...] = 4.0 * loose + SCALE * pull[...]
+
+    @pl.when(has_next)
+    def _():
+        lax.fori_loop(late, chunks, correlate, 0)
 
     pl.when(has_above)(lambda: flow_copy(True).start())
     pl.when(has_below)(lambda: flow_copy(False).start())
@@ -471,9 +497,10 @@
             pltpu.SemaphoreType.DMA((2,)),
             pltpu.SemaphoreType.DMA((bands - 1,)),
             pltpu.SemaphoreType.DMA((bands - 1,)),
+            pltpu.SemaphoreType.REGULAR((2,)),
         ],
         compiler_params=pltpu.CompilerParams(
-            collective_id=0, has_side_effects=True, vmem_limit_bytes=40 * 1024 * 1024
+            collective_id=0, has_side_effects=True, vmem_limit_bytes=60 * 1024 * 1024
         ),
         cost_estimate=pl.CostEstimate(flops=2_400_000_000, bytes_accessed=4_000_000, transcendentals=0),
     )(image, tissue_mask, anchor, fixed_nodes, prior_shift, jnp.asarray(both), jnp.asarray(narrow))

time: 66.7 us -> 51.9 us (0.78)
  the two profiles are of different devices: /device:TPU:337 before, /device:TPU:217 now
where the time goes in v2:
time: 51.9 us; the launch traced here: 51.8 us
  Pallas kernels  50.1 us (97%)
  local copies, waits for them, and re-layouts  1.67 us (3%)
    pallas_call x1, Pallas kernels, per_device(): pl.pallas_call(functools.partial(kernel, sections, bands), out_shape=jax....  50.1 us
    unnamed x1, local copies, waits for them, and re-layouts  1.67 us

profile of v2, /device:TPU:217, one launch (start us, length us, event | category | flops | bytes accessed | tf_op | source)
XLA Modules:
  0.0 51.8 jit_solution(8535379598501981785)
XLA Ops:
  0.0 50.1 %shard_map.73 = f32[2,32,1024]{2,1,0:T(8,128)} custom-call(bf16[1,128,4096]{2,1,0:T(8,128)(2,1)} %image_hbm.1, s32[1,128,4096]{2,1,0:T(8,128)} %mask_hbm.1, f32[1,32,1024]{2,1,0:T(8,128)} %anchor_hbm.1, s32[1,32,1024]{2,1,0:T(8,128)} %fixed_hbm.1, f32[2,1,32,1024]{3,2,1,0:T(8,128)} %prior_hbm.1, bf16[256,256]{1,0:T(8,128)(2,1)} %constant.4.clone.both_hbm, ...), custom_call_target="tpu_custom_call" | custom-call | flops 2400000000 | bytes 4000000 | tf_op jit(solution)/shard_map/pallas_call | solution.py:463
  50.1 1.7 %copy.10 = f32[2,1,32,1024]{3,2,1,0:T(8,128)} copy(f32[2,1,32,1024]{3,2,1,0:T(8,128)} %bitcast.3) | data formatting | bytes 524288

commit v3 on v2

--- a/solution.py
+++ b/solution.py
@@ -460,6 +460,8 @@
     wide = 2 * EDGE + rows
     width = 3 * nodes // 4
     both, narrow = tables()
+    operands = image, tissue_mask, anchor, fixed_nodes, prior_shift, jnp.asarray(both), jnp.asarray(narrow)
+    operands = [pltpu.with_memory_space_constraint(operand, pltpu.HBM) for operand in operands]
     out = pl.pallas_call(
         functools.partial(kernel, sections, bands),
         out_shape=jax.ShapeDtypeStruct((2, rows, nodes), jnp.float32),
@@ -500,10 +502,10 @@
             pltpu.SemaphoreType.REGULAR((2,)),
         ],
         compiler_params=pltpu.CompilerParams(
-            collective_id=0, has_side_effects=True, vmem_limit_bytes=60 * 1024 * 1024
+            collective_id=0, has_side_effects=True, vmem_limit_bytes=40 * 1024 * 1024
         ),
         cost_estimate=pl.CostEstimate(flops=2_400_000_000, bytes_accessed=4_000_000, transcendentals=0),
-    )(image, tissue_mask, anchor, fixed_nodes, prior_shift, jnp.asarray(both), jnp.asarray(narrow))
+    )(*operands)
     return out[:, None]
 
 

time: 51.9 us -> 50.2 us (0.967)
  local copies, waits for them, and re-layouts: 1.67 us -> 0.71 us
  Pallas kernels: 50.1 us -> 49.4 us
    unnamed x1, local copies, waits for them, and re-layouts: 1.67 us -> 0.71 us
    pallas_call x1, Pallas kernels: 50.1 us -> 49.4 us  [per_device(): pl.pallas_call(functools.partial(kernel, sections, bands), out_shape=jax....]
where the time goes in v3:
time: 50.2 us; the launch traced here: 50.1 us
  Pallas kernels  49.4 us (98%)
  local copies, waits for them, and re-layouts  0.71 us (1%)
    pallas_call x1, Pallas kernels, per_device(): pl.pallas_call(functools.partial(kernel, sections, bands), out_shape=jax....  49.4 us

profile of v3, /device:TPU:217, one launch (start us, length us, event | category | flops | bytes accessed | tf_op | source)
XLA Modules:
  0.0 50.1 jit_solution(9933632087593520596)
XLA Ops:
  0.0 49.4 %shard_map.73 = f32[2,32,1024]{2,1,0:T(8,128)S(1)} custom-call(bf16[1,128,4096]{2,1,0:T(8,128)(2,1)} %image_hbm.1, s32[1,128,4096]{2,1,0:T(8,128)} %mask_hbm.1, f32[1,32,1024]{2,1,0:T(8,128)} %anchor_hbm.1, s32[1,32,1024]{2,1,0:T(8,128)} %fixed_hbm.1, f32[2,1,32,1024]{3,2,1,0:T(8,128)} %prior_hbm.1, bf16[256,256]{1,0:T(8,128)(2,1)} %constant.4.clone.both_hbm, ...), custom_call_target="tpu_custom_call" | custom-call | flops 2400000000 | bytes 4000000 | tf_op jit(solution)/shard_map/pallas_call | solution.py:465
  49.4 0.7 %copy.10 = f32[2,1,32,1024]{3,2,1,0:T(8,128)} copy(f32[2,1,32,1024]{3,2,1,0:T(8,128)S(1)} %bitcast.3) | data formatting | bytes 524288

commit v4 on v3

--- a/solution.py
+++ b/solution.py
@@ -17,7 +17,8 @@
 LANES = 128
 EDGE = 8
 SPAN = 4
-SHIFTS = (1.0, 4.0, 1.0, 4.0)
+REACH = 2 * ITERS - 1
+SHIFTS = (1.0, 4.0, 1.0, 4.0, 1.0, 4.0, 1.0)
 SCALE = 0.25
 PAIRS = tuple((i, j) for i in range(ITERS) for j in range(i, ITERS)) + tuple((i, ITERS) for i in range(ITERS))
 
@@ -134,15 +135,20 @@
     anchor,
     fixed,
     prior,
-    edge_out,
-    edge_in,
+    edge_up,
+    edge_down,
+    from_below,
+    from_above,
     pull,
     diag,
     link,
     base,
     flow,
     flow_in,
+    listed,
+    pick,
     basis,
+    whole,
     share,
     shares,
     load_sem,
@@ -243,8 +249,8 @@
     def edge_copy(up):
         slot = 0 if up else 1
         return pltpu.make_async_remote_copy(
-            edge_out.at[slot],
-            edge_in.at[slot],
+            edge_up if up else edge_down,
+            from_below if up else from_above,
             edge_send.at[slot],
             edge_recv.at[slot],
             device_id={"blk": blk - 1 if up else blk + 1},
@@ -262,19 +268,23 @@
             device_id_type=MESH,
         )
 
-    width = 3 * tiles * LANES // 4
-
-    def packed(first):
-        flat = jnp.concatenate([part[first : first + SPAN] for part in own], axis=1)
+    nodes = tiles * LANES
+
+    def packed(first, count):
+        flat = [part[at : at + SPAN] for part in own for at in range(first, first + count, SPAN)]
+        flat = jnp.concatenate(flat, axis=1)
+        width = flat.shape[1] // 4
         return jnp.concatenate([flat[:, k * width : (k + 1) * width] for k in range(4)], axis=0).astype(jnp.bfloat16)
 
     def unpacked(block):
         block = block.astype(jnp.float32)
         flat = jnp.concatenate([block[k * SPAN : (k + 1) * SPAN] for k in range(4)], axis=1)
-        return [flat[:, k * tiles * LANES : (k + 1) * tiles * LANES] for k in range(3)]
-
-    edge_out[0] = packed(0)
-    edge_out[1] = packed(rows - SPAN)
+        parts = [flat[:, k : k + nodes] for k in range(0, flat.shape[1], nodes)]
+        each = len(parts) // 3
+        return [parts[k * each : (k + 1) * each] for k in range(3)]
+
+    edge_up[...] = packed(0, EDGE)
+    edge_down[...] = packed(rows - SPAN, SPAN)
     greeted = has_prev, has_next, has_above, has_below
     pl.semaphore_wait(barrier, turns + 1 + functools.reduce(lambda p, q: p + q, [g.astype(jnp.int32) for g in greeted]))
     pl.when(has_above)(lambda: edge_copy(True).start())
@@ -301,15 +311,24 @@
         base[0, g, EDGE : EDGE + rows] = own[1][:, at]
         base[1, g, EDGE : EDGE + rows] = own[2][:, at]
 
-    def take_edge(slot, first):
-        parts = unpacked(edge_in[slot])
-        for g in range(tiles):
-            at = slice(g * LANES, (g + 1) * LANES)
-            pull[g, first : first + SPAN] = parts[0][:, at]
-            base[0, g, first : first + SPAN] = parts[1][:, at]
-            base[1, g, first : first + SPAN] = parts[2][:, at]
+    def take_edge(block, first, count):
+        parts = unpacked(block)
+        for n in range(0, count, SPAN):
+            some = min(SPAN, count - n)
+            to = slice(first + n, first + n + some)
+            for g in range(tiles):
+                at = slice(g * LANES, (g + 1) * LANES)
+                pull[g, to] = parts[0][n // SPAN][:some, at]
+                base[0, g, to] = parts[1][n // SPAN][:some, at]
+                base[1, g, to] = parts[2][n // SPAN][:some, at]
 
     flow[...] = jnp.zeros_like(flow)
+    listed[...] = jnp.zeros_like(listed)
+    lane = lax.broadcasted_iota(jnp.int32, (8, LANES), 1)
+    patch = lax.broadcasted_iota(jnp.int32, (nodes, LANES), 0) // (LANES // 4)
+    for k in range(2):
+        column = lax.broadcasted_iota(jnp.int32, (nodes, LANES), 1)
+        pick[k] = jnp.where(column == patch + k * (LANES // 4), 1.0, 0.0).astype(jnp.bfloat16)
     tile_row = lax.broadcasted_iota(jnp.int32, (tiles, LANES), 0)
     quarter = lax.broadcasted_iota(jnp.int32, (tiles, LANES), 1) // (LANES // 4)
 
@@ -319,6 +338,8 @@
         for k, value in enumerate(flows_of(spectra[c], other, narrow[...], both[...])):
             held = flow[k]
             for p in range(2):
+                slot = lane == k * (LANES // 4) + 2 * c + p
+                listed[...] = jnp.where(slot, value[p : p + 1], listed[...])
                 spot = (tile_row == c // 2) & (quarter == 2 * (c % 2) + p)
                 held = jnp.where(spot, value[p : p + 1], held)
             flow[k] = held
@@ -333,12 +354,12 @@
     @pl.when(has_below)
     def _():
         edge_copy(True).wait_recv()
-        take_edge(0, EDGE + rows)
+        take_edge(from_below[...], EDGE + rows, REACH)
 
     @pl.when(has_above)
     def _():
         edge_copy(False).wait_recv()
-        take_edge(1, EDGE - SPAN)
+        take_edge(from_above[...], EDGE - SPAN, SPAN)
 
     loose = jnp.where(pull[...] > 0.0, SCALE, 0.0)
     link[...] = loose
@@ -351,53 +372,62 @@
     pl.when(has_above)(lambda: flow_copy(True).start())
     pl.when(has_below)(lambda: flow_copy(False).start())
 
-    @pl.when(has_below)
-    def _():
-        flow_copy(True).wait_recv()
-
-    @pl.when(has_above)
-    def _():
-        flow_copy(False).wait_recv()
-
-    @pl.when(jnp.logical_not(has_below))
-    def _():
-        flow_in[0] = jnp.zeros_like(flow)
-
-    @pl.when(jnp.logical_not(has_above))
-    def _():
-        flow_in[1] = jnp.zeros_like(flow)
-
+    def advance(value, step, at=slice(None)):
+        return (diag[:, at] - SCALE * SHIFTS[step]) * value - link[:, at] * neighbours(value)
+
+    part = lane // (LANES // 4)
+    sums, strips, priors = [], [], []
+    below = slice(EDGE + rows, EDGE + rows + EDGE)
+    tail = slice(rows, rows + 2 * EDGE)
     for k in range(2):
         for g in range(tiles):
-            for source, first, count in (
-                (flow_in.at[1], 0, EDGE),
-                (flow, EDGE, rows),
-                (flow_in.at[0], EDGE + rows, EDGE),
-            ):
-                at = slice(first, first + count)
-                basis[k, 0, g, at] = base[k, g, at] + pull[g, at] * source[k, g : g + 1, :]
-
-    lane = lax.broadcasted_iota(jnp.int32, (8, LANES), 1)
-    sums = []
-    for k in range(2):
+            inner = slice(EDGE, EDGE + rows)
+            basis[k, 0, g, :EDGE] = jnp.zeros((EDGE, LANES), jnp.float32)
+            basis[k, 0, g, inner] = base[k, g, inner] + pull[g, inner] * flow[k, g : g + 1, :]
+            basis[k, 0, g, below] = jnp.zeros((EDGE, LANES), jnp.float32)
         for step in range(ITERS):
-            value = basis[k, step]
-            basis[k, step + 1] = (diag[...] - SCALE * SHIFTS[step]) * value - link[...] * neighbours(value)
+            basis[k, step + 1] = advance(basis[k, step], step)
         lines = []
         for i, j in PAIRS:
-            product = basis[k, i, :, EDGE : EDGE + rows] * basis[k, j, :, EDGE : EDGE + rows]
-            total = jnp.sum(product.reshape(tiles * rows // 8, 8, LANES), axis=0)
+            product = basis[k, i] * basis[k, j]
+            total = jnp.sum(product.reshape(tiles * (rows + 2 * EDGE) // 8, 8, LANES), axis=0)
             lines.append(jnp.sum(total, axis=0, keepdims=True))
         lines += [jnp.zeros((1, LANES), jnp.float32)] * (16 - len(lines))
         for half in range(2):
             block = jnp.concatenate(lines[8 * half : 8 * half + 8], axis=0)
             block = block + pltpu.roll(block, LANES // 2, 1)
             sums.append(block + pltpu.roll(block, LANES // 4, 1))
-    part = lane // (LANES // 4)
+        reached = [basis[k, step][:, below] for step in range(1, ITERS + 1)]
+        value = basis[k, ITERS][:, tail]
+        for step in range(ITERS, REACH):
+            value = advance(value, step, tail)
+            reached.append(value[:, EDGE:])
+        strip, line = [], [jnp.zeros((1, LANES), jnp.float32)]
+        for value in reached:
+            weighted = pull[:, below] * value
+            strip.append(jnp.concatenate([weighted[g] for g in range(tiles)], axis=1))
+            line.append(jnp.sum(jnp.sum(base[k, :, below] * value, axis=0), axis=0, keepdims=True))
+        strips.append(jnp.concatenate(strip, axis=0))
+        block = jnp.concatenate(line, axis=0)
+        block = block + pltpu.roll(block, LANES // 2, 1)
+        priors.append(block + pltpu.roll(block, LANES // 4, 1))
     mine = sums[3]
     for n in range(3):
         mine = jnp.where(part == n, sums[n], mine)
-    share[...] = mine
+    share[8:] = mine
+
+    gathered = jnp.zeros((REACH * EDGE, LANES), jnp.float32)
+    for k in range(2):
+        left = strips[k]
+        for _ in range(3):
+            piece = left.astype(jnp.bfloat16)
+            gathered = gathered + matmul(piece, pick[k])
+            left = left - piece.astype(jnp.float32)
+    gathered = jnp.sum(gathered.reshape(REACH, EDGE, LANES), axis=1)
+    gathered = jnp.concatenate([jnp.zeros((1, LANES), jnp.float32), gathered], axis=0)
+    crossing = 2.0 * jnp.where(part < 2, gathered, jnp.where(part == 2, priors[0], priors[1]))
+    first = lax.broadcasted_iota(jnp.int32, (8, LANES), 0) == 0
+    share[:8] = jnp.where(first, listed[...], crossing)
 
     def share_copy(n):
         return pltpu.make_async_remote_copy(
@@ -412,22 +442,61 @@
     for n in range(bands - 1):
         share_copy(n).start()
     shares[blk] = share[...]
+
+    @pl.when(has_below)
+    def _():
+        flow_copy(True).wait_recv()
+
+    @pl.when(has_above)
+    def _():
+        flow_copy(False).wait_recv()
+
+    @pl.when(jnp.logical_not(has_below))
+    def _():
+        flow_in[0] = jnp.zeros_like(flow)
+
+    @pl.when(jnp.logical_not(has_above))
+    def _():
+        flow_in[1] = jnp.zeros_like(flow)
+
+    for k in range(2):
+        for g in range(tiles):
+            for source, first_row, count in (
+                (flow_in.at[1], 0, EDGE),
+                (flow, EDGE, rows),
+                (flow_in.at[0], EDGE + rows, EDGE),
+            ):
+                at = slice(first_row, first_row + count)
+                whole[k, 0, g, at] = base[k, g, at] + pull[g, at] * source[k, g : g + 1, :]
+        for step in range(ITERS - 1):
+            whole[k, step + 1] = advance(whole[k, step], step)
+
     for n in range(bands - 1):
         share_copy(n).wait_recv()
-    total = jnp.sum(shares[...], axis=0)
+    total = jnp.sum(shares[:, 8:], axis=0)
     quarters = [jnp.sum(jnp.where(part == n, total, 0.0), axis=1, keepdims=True) for n in range(4)]
+    crossed = jnp.zeros((8, LANES), jnp.float32)
+    for n in range(bands - 1):
+        crossed = crossed + shares[n, :8] * jnp.where(lane[:1] < LANES // 2, shares[n + 1, :1], 1.0)
+    halves = [jnp.sum(jnp.where(part % 2 == k, crossed, 0.0), axis=1, keepdims=True) for k in range(2)]
+    halves = [jnp.where(lane[:1] < LANES // 2, halves[0][m : m + 1], halves[1][m : m + 1]) for m in range(REACH + 1)]
     gram = {}
     for n, pair in enumerate(PAIRS):
         line = [quarters[2 * k + n // 8][n % 8 : n % 8 + 1] for k in range(2)]
         gram[pair] = jnp.where(lane[:1] < LANES // 2, line[0], line[1])
+        degree = sum(pair)
+        if degree:
+            gram[pair] = gram[pair] + halves[degree]
+        if pair[0] % 2 and pair[1] % 2:
+            gram[pair] = gram[pair] + SCALE * (SHIFTS[1] - SHIFTS[0]) * halves[degree - 1]
     found = coefficients(gram)
     for k in range(2):
         weights = [value[:, k * LANES // 2 : k * LANES // 2 + 1] for value in found]
         for g in range(tiles):
             at = slice(EDGE, EDGE + rows)
-            value = weights[0] * basis[k, 0, g, at]
+            value = weights[0] * whole[k, 0, g, at]
             for step in range(1, ITERS):
-                value = value + weights[step] * basis[k, step, g, at]
+                value = value + weights[step] * whole[k, step, g, at]
             out_ref[k, :, g * LANES : (g + 1) * LANES] = value
 
     for n in range(bands - 1):
@@ -478,17 +547,22 @@
             pltpu.VMEM((rows, nodes), jnp.float32),
             pltpu.VMEM((rows, nodes), jnp.int32),
             pltpu.VMEM((2, rows, nodes), jnp.float32),
-            pltpu.VMEM((2, 4 * SPAN, width), jnp.bfloat16),
-            pltpu.VMEM((2, 4 * SPAN, width), jnp.bfloat16),
+            pltpu.VMEM((4 * SPAN, 2 * width), jnp.bfloat16),
+            pltpu.VMEM((4 * SPAN, width), jnp.bfloat16),
+            pltpu.VMEM((4 * SPAN, 2 * width), jnp.bfloat16),
+            pltpu.VMEM((4 * SPAN, width), jnp.bfloat16),
             pltpu.VMEM((tiles, wide, LANES), jnp.float32),
             pltpu.VMEM((tiles, wide, LANES), jnp.float32),
             pltpu.VMEM((tiles, wide, LANES), jnp.float32),
             pltpu.VMEM((2, tiles, wide, LANES), jnp.float32),
             pltpu.VMEM((2, tiles, LANES), jnp.float32),
             pltpu.VMEM((2, 2, tiles, LANES), jnp.float32),
+            pltpu.VMEM((8, LANES), jnp.float32),
+            pltpu.VMEM((2, nodes, LANES), jnp.bfloat16),
             pltpu.VMEM((2, ITERS + 1, tiles, wide, LANES), jnp.float32),
-            pltpu.VMEM((8, LANES), jnp.float32),
-            pltpu.VMEM((bands, 8, LANES), jnp.float32),
+            pltpu.VMEM((2, ITERS, tiles, wide, LANES), jnp.float32),
+            pltpu.VMEM((16, LANES), jnp.float32),
+            pltpu.VMEM((bands, 16, LANES), jnp.float32),
             pltpu.SemaphoreType.DMA((2, chunks)),
             pltpu.SemaphoreType.DMA((5,)),
             pltpu.SemaphoreType.DMA((chunks,)),

time: 50.2 us -> 46.9 us (0.934)
  the two profiles are of different devices: /device:TPU:217 before, /device:TPU:248 now
where the time goes in v4:
time: 46.9 us; the launch traced here: 46.8 us
  Pallas kernels  46.1 us (98%)
  local copies, waits for them, and re-layouts  0.71 us (2%)
    pallas_call x1, Pallas kernels, per_device(): pl.pallas_call(functools.partial(kernel, sections, bands), out_shape=jax....  46.1 us

profile of v4, /device:TPU:248, one launch (start us, length us, event | category | flops | bytes accessed | tf_op | source)
XLA Modules:
  0.0 46.8 jit_solution(1850066561670510479)
XLA Ops:
  0.0 46.1 %shard_map.73 = f32[2,32,1024]{2,1,0:T(8,128)S(1)} custom-call(bf16[1,128,4096]{2,1,0:T(8,128)(2,1)} %image_hbm.1, s32[1,128,4096]{2,1,0:T(8,128)} %mask_hbm.1, f32[1,32,1024]{2,1,0:T(8,128)} %anchor_hbm.1, s32[1,32,1024]{2,1,0:T(8,128)} %fixed_hbm.1, f32[2,1,32,1024]{3,2,1,0:T(8,128)} %prior_hbm.1, bf16[256,256]{1,0:T(8,128)(2,1)} %constant.4.clone.both_hbm, ...), custom_call_target="tpu_custom_call" | custom-call | flops 2400000000 | bytes 4000000 | tf_op jit(solution)/shard_map/pallas_call | solution.py:534
  46.1 0.7 %copy.10 = f32[2,1,32,1024]{3,2,1,0:T(8,128)} copy(f32[2,1,32,1024]{3,2,1,0:T(8,128)S(1)} %bitcast.3) | data formatting | bytes 524288

commit v5 on v4

--- a/solution.py
+++ b/solution.py
@@ -148,6 +148,7 @@
     listed,
     pick,
     basis,
+    reach,
     whole,
     share,
     shares,
@@ -345,11 +346,12 @@
             flow[k] = held
         return 0
 
-    late = chunks * 3 // 4
+    pause = chunks - 4
+    known = pause * PAIR // SIZE // 4
 
     @pl.when(has_next)
     def _():
-        lax.fori_loop(0, late, correlate, 0)
+        lax.fori_loop(0, pause, correlate, 0)
 
     @pl.when(has_below)
     def _():
@@ -365,69 +367,80 @@
     link[...] = loose
     diag[...] = 4.0 * loose + SCALE * pull[...]
 
+    part = lane // (LANES // 4)
+    below = slice(EDGE + rows, EDGE + rows + EDGE)
+    tail = slice(rows, rows + 2 * EDGE)
+
+    def advance(value, step, tile=slice(None), at=slice(None), kept=0):
+        return (diag[tile, at] - SCALE * SHIFTS[step]) * value[kept:] - link[tile, at] * neighbours(value)[kept:]
+
+    def own_basis(first, last, kept):
+        new, read = slice(first + kept, last), slice(first, last)
+        for k in range(2):
+            for g in range(first + kept, last):
+                inner = slice(EDGE, EDGE + rows)
+                basis[k, 0, g, :EDGE] = jnp.zeros((EDGE, LANES), jnp.float32)
+                basis[k, 0, g, inner] = base[k, g, inner] + pull[g, inner] * flow[k, g : g + 1, :]
+                basis[k, 0, g, below] = jnp.zeros((EDGE, LANES), jnp.float32)
+            for step in range(ITERS):
+                basis[k, step + 1, new] = advance(basis[k, step, read], step, new, slice(None), kept)
+            for step in range(ITERS, REACH):
+                value = basis[k, step, read, tail] if step == ITERS else reach[k, step - ITERS - 1, read]
+                reach[k, step - ITERS, new] = advance(value, step, new, tail, kept)
+
+    def own_sums(first, last):
+        count = last - first
+        over = slice(first, last)
+        blocks = []
+        gathered = jnp.zeros((REACH * EDGE, LANES), jnp.float32)
+        for k in range(2):
+            lines = []
+            for i, j in PAIRS:
+                product = basis[k, i, over] * basis[k, j, over]
+                total = jnp.sum(product.reshape(count * (rows + 2 * EDGE) // 8, 8, LANES), axis=0)
+                lines.append(jnp.sum(total, axis=0, keepdims=True))
+            lines += [jnp.zeros((1, LANES), jnp.float32)] * (16 - len(lines))
+            reached = [basis[k, step, over, below] for step in range(1, ITERS + 1)]
+            reached += [reach[k, step, over, EDGE:] for step in range(REACH - ITERS)]
+            strip = []
+            lines.append(jnp.zeros((1, LANES), jnp.float32))
+            for value in reached:
+                weighted = pull[over, below] * value
+                strip.append(jnp.concatenate([weighted[g] for g in range(count)], axis=1))
+                lines.append(jnp.sum(jnp.sum(base[k, over, below] * value, axis=0), axis=0, keepdims=True))
+            blocks += [jnp.concatenate(lines[n : n + 8], axis=0) for n in (0, 8, 16)]
+            left = jnp.concatenate(strip, axis=0)
+            for _ in range(3):
+                piece = left.astype(jnp.bfloat16)
+                gathered = gathered + matmul(piece, pick[k, first * LANES : last * LANES])
+                left = left - piece.astype(jnp.float32)
+        gathered = jnp.sum(gathered.reshape(REACH, EDGE, LANES), axis=1)
+        return blocks + [jnp.concatenate([jnp.zeros((1, LANES), jnp.float32), gathered], axis=0)]
+
+    def folded(block):
+        block = block + pltpu.roll(block, LANES // 2, 1)
+        return block + pltpu.roll(block, LANES // 4, 1)
+
+    own_basis(0, known, 0)
+    early = own_sums(0, known - 1)
+
     @pl.when(has_next)
     def _():
-        lax.fori_loop(late, chunks, correlate, 0)
+        lax.fori_loop(pause, chunks, correlate, 0)
 
     pl.when(has_above)(lambda: flow_copy(True).start())
     pl.when(has_below)(lambda: flow_copy(False).start())
-
-    def advance(value, step, at=slice(None)):
-        return (diag[:, at] - SCALE * SHIFTS[step]) * value - link[:, at] * neighbours(value)
-
-    part = lane // (LANES // 4)
-    sums, strips, priors = [], [], []
-    below = slice(EDGE + rows, EDGE + rows + EDGE)
-    tail = slice(rows, rows + 2 * EDGE)
-    for k in range(2):
-        for g in range(tiles):
-            inner = slice(EDGE, EDGE + rows)
-            basis[k, 0, g, :EDGE] = jnp.zeros((EDGE, LANES), jnp.float32)
-            basis[k, 0, g, inner] = base[k, g, inner] + pull[g, inner] * flow[k, g : g + 1, :]
-            basis[k, 0, g, below] = jnp.zeros((EDGE, LANES), jnp.float32)
-        for step in range(ITERS):
-            basis[k, step + 1] = advance(basis[k, step], step)
-        lines = []
-        for i, j in PAIRS:
-            product = basis[k, i] * basis[k, j]
-            total = jnp.sum(product.reshape(tiles * (rows + 2 * EDGE) // 8, 8, LANES), axis=0)
-            lines.append(jnp.sum(total, axis=0, keepdims=True))
-        lines += [jnp.zeros((1, LANES), jnp.float32)] * (16 - len(lines))
-        for half in range(2):
-            block = jnp.concatenate(lines[8 * half : 8 * half + 8], axis=0)
-            block = block + pltpu.roll(block, LANES // 2, 1)
-            sums.append(block + pltpu.roll(block, LANES // 4, 1))
-        reached = [basis[k, step][:, below] for step in range(1, ITERS + 1)]
-        value = basis[k, ITERS][:, tail]
-        for step in range(ITERS, REACH):
-            value = advance(value, step, tail)
-            reached.append(value[:, EDGE:])
-        strip, line = [], [jnp.zeros((1, LANES), jnp.float32)]
-        for value in reached:
-            weighted = pull[:, below] * value
-            strip.append(jnp.concatenate([weighted[g] for g in range(tiles)], axis=1))
-            line.append(jnp.sum(jnp.sum(base[k, :, below] * value, axis=0), axis=0, keepdims=True))
-        strips.append(jnp.concatenate(strip, axis=0))
-        block = jnp.concatenate(line, axis=0)
-        block = block + pltpu.roll(block, LANES // 2, 1)
-        priors.append(block + pltpu.roll(block, LANES // 4, 1))
+    own_basis(known - 2, tiles, 1)
+    blocks = [p + q for p, q in zip(early, own_sums(known - 1, tiles))]
+    sums = [folded(blocks[n]) for n in (0, 1, 3, 4)]
+    priors = [folded(blocks[n]) for n in (2, 5)]
     mine = sums[3]
     for n in range(3):
         mine = jnp.where(part == n, sums[n], mine)
     share[8:] = mine
-
-    gathered = jnp.zeros((REACH * EDGE, LANES), jnp.float32)
-    for k in range(2):
-        left = strips[k]
-        for _ in range(3):
-            piece = left.astype(jnp.bfloat16)
-            gathered = gathered + matmul(piece, pick[k])
-            left = left - piece.astype(jnp.float32)
-    gathered = jnp.sum(gathered.reshape(REACH, EDGE, LANES), axis=1)
-    gathered = jnp.concatenate([jnp.zeros((1, LANES), jnp.float32), gathered], axis=0)
-    crossing = 2.0 * jnp.where(part < 2, gathered, jnp.where(part == 2, priors[0], priors[1]))
-    first = lax.broadcasted_iota(jnp.int32, (8, LANES), 0) == 0
-    share[:8] = jnp.where(first, listed[...], crossing)
+    crossing = 2.0 * jnp.where(part < 2, blocks[6], jnp.where(part == 2, priors[0], priors[1]))
+    top = lax.broadcasted_iota(jnp.int32, (8, LANES), 0) == 0
+    share[:8] = jnp.where(top, listed[...], crossing)
 
     def share_copy(n):
         return pltpu.make_async_remote_copy(
@@ -560,6 +573,7 @@
             pltpu.VMEM((8, LANES), jnp.float32),
             pltpu.VMEM((2, nodes, LANES), jnp.bfloat16),
             pltpu.VMEM((2, ITERS + 1, tiles, wide, LANES), jnp.float32),
+            pltpu.VMEM((2, REACH - ITERS, tiles, 2 * EDGE, LANES), jnp.float32),
             pltpu.VMEM((2, ITERS, tiles, wide, LANES), jnp.float32),
             pltpu.VMEM((16, LANES), jnp.float32),
             pltpu.VMEM((bands, 16, LANES), jnp.float32),

time: 46.9 us -> 46.1 us (0.983)
  Pallas kernels: 46.1 us -> 45.2 us
    pallas_call x1, Pallas kernels: 46.1 us -> 45.2 us  [per_device(): pl.pallas_call(functools.partial(kernel, sections, bands), out_shape=jax....]
where the time goes in v5:
time: 46.1 us; the launch traced here: 45.9 us
  Pallas kernels  45.2 us (98%)
  local copies, waits for them, and re-layouts  0.71 us (2%)
    pallas_call x1, Pallas kernels, per_device(): pl.pallas_call(functools.partial(kernel, sections, bands), out_shape=jax....  45.2 us

profile of v5, /device:TPU:248, one launch (start us, length us, event | category | flops | bytes accessed | tf_op | source)
XLA Modules:
  0.0 45.9 jit_solution(9645473592835221588)
XLA Ops:
  0.0 45.2 %shard_map.73 = f32[2,32,1024]{2,1,0:T(8,128)S(1)} custom-call(bf16[1,128,4096]{2,1,0:T(8,128)(2,1)} %image_hbm.1, s32[1,128,4096]{2,1,0:T(8,128)} %mask_hbm.1, f32[1,32,1024]{2,1,0:T(8,128)} %anchor_hbm.1, s32[1,32,1024]{2,1,0:T(8,128)} %fixed_hbm.1, f32[2,1,32,1024]{3,2,1,0:T(8,128)} %prior_hbm.1, bf16[256,256]{1,0:T(8,128)(2,1)} %constant.4.clone.both_hbm, ...), custom_call_target="tpu_custom_call" | custom-call | flops 2400000000 | bytes 4000000 | tf_op jit(solution)/shard_map/pallas_call | solution.py:547
  45.2 0.7 %copy.10 = f32[2,1,32,1024]{3,2,1,0:T(8,128)} copy(f32[2,1,32,1024]{3,2,1,0:T(8,128)S(1)} %bitcast.3) | data formatting | bytes 524288

commit v6 on v5

--- a/solution.py
+++ b/solution.py
@@ -86,6 +86,13 @@
     left = pltpu.roll(value, LANES - 1, 2)
     left = jnp.where(lane == LANES - 1, jnp.concatenate([left[1:], none], axis=0), left)
     return pltpu.roll(value, 1, 1) + pltpu.roll(value, rows - 1, 1) + right + left
+
+
+def crossed(pair, powers):
+    degree = sum(pair)
+    if pair[0] % 2 and pair[1] % 2:
+        return powers[degree] + SCALE * (SHIFTS[1] - SHIFTS[0]) * powers[degree - 1]
+    return powers[degree]
 
 
 def coefficients(gram):
@@ -367,7 +374,7 @@
     link[...] = loose
     diag[...] = 4.0 * loose + SCALE * pull[...]
 
-    part = lane // (LANES // 4)
+    part = lane // (LANES // 8)
     below = slice(EDGE + rows, EDGE + rows + EDGE)
     tail = slice(rows, rows + 2 * EDGE)
 
@@ -399,16 +406,16 @@
                 product = basis[k, i, over] * basis[k, j, over]
                 total = jnp.sum(product.reshape(count * (rows + 2 * EDGE) // 8, 8, LANES), axis=0)
                 lines.append(jnp.sum(total, axis=0, keepdims=True))
-            lines += [jnp.zeros((1, LANES), jnp.float32)] * (16 - len(lines))
             reached = [basis[k, step, over, below] for step in range(1, ITERS + 1)]
             reached += [reach[k, step, over, EDGE:] for step in range(REACH - ITERS)]
-            strip = []
-            lines.append(jnp.zeros((1, LANES), jnp.float32))
+            strip, prior_lines = [], [jnp.zeros((1, LANES), jnp.float32)]
             for value in reached:
                 weighted = pull[over, below] * value
                 strip.append(jnp.concatenate([weighted[g] for g in range(count)], axis=1))
-                lines.append(jnp.sum(jnp.sum(base[k, over, below] * value, axis=0), axis=0, keepdims=True))
-            blocks += [jnp.concatenate(lines[n : n + 8], axis=0) for n in (0, 8, 16)]
+                prior_lines.append(2.0 * jnp.sum(jnp.sum(base[k, over, below] * value, axis=0), axis=0, keepdims=True))
+            lines = [line + crossed(pair, prior_lines) for line, pair in zip(lines, PAIRS)]
+            lines += [jnp.zeros((1, LANES), jnp.float32)] * (16 - len(lines))
+            blocks += [jnp.concatenate(lines[n : n + 8], axis=0) for n in (0, 8)]
             left = jnp.concatenate(strip, axis=0)
             for _ in range(3):
                 piece = left.astype(jnp.bfloat16)
@@ -418,8 +425,9 @@
         return blocks + [jnp.concatenate([jnp.zeros((1, LANES), jnp.float32), gathered], axis=0)]
 
     def folded(block):
-        block = block + pltpu.roll(block, LANES // 2, 1)
-        return block + pltpu.roll(block, LANES // 4, 1)
+        for lanes in (LANES // 2, LANES // 4, LANES // 8):
+            block = block + pltpu.roll(block, lanes, 1)
+        return block
 
     own_basis(0, known, 0)
     early = own_sums(0, known - 1)
@@ -432,15 +440,11 @@
     pl.when(has_below)(lambda: flow_copy(False).start())
     own_basis(known - 2, tiles, 1)
     blocks = [p + q for p, q in zip(early, own_sums(known - 1, tiles))]
-    sums = [folded(blocks[n]) for n in (0, 1, 3, 4)]
-    priors = [folded(blocks[n]) for n in (2, 5)]
-    mine = sums[3]
-    for n in range(3):
-        mine = jnp.where(part == n, sums[n], mine)
-    share[8:] = mine
-    crossing = 2.0 * jnp.where(part < 2, blocks[6], jnp.where(part == 2, priors[0], priors[1]))
+    mine = 2.0 * blocks[4]
+    for n in range(4):
+        mine = jnp.where(part == 4 + n, folded(blocks[n]), mine)
     top = lax.broadcasted_iota(jnp.int32, (8, LANES), 0) == 0
-    share[:8] = jnp.where(top, listed[...], crossing)
+    share[...] = jnp.where(top & (part < 4), listed[...], mine)
 
     def share_copy(n):
         return pltpu.make_async_remote_copy(
@@ -486,22 +490,21 @@
 
     for n in range(bands - 1):
         share_copy(n).wait_recv()
-    total = jnp.sum(shares[:, 8:], axis=0)
-    quarters = [jnp.sum(jnp.where(part == n, total, 0.0), axis=1, keepdims=True) for n in range(4)]
-    crossed = jnp.zeros((8, LANES), jnp.float32)
+    total = shares[bands - 1]
     for n in range(bands - 1):
-        crossed = crossed + shares[n, :8] * jnp.where(lane[:1] < LANES // 2, shares[n + 1, :1], 1.0)
-    halves = [jnp.sum(jnp.where(part % 2 == k, crossed, 0.0), axis=1, keepdims=True) for k in range(2)]
-    halves = [jnp.where(lane[:1] < LANES // 2, halves[0][m : m + 1], halves[1][m : m + 1]) for m in range(REACH + 1)]
+        total = total + shares[n] * jnp.where(lane[:1] < LANES // 2, shares[n + 1, :1], 1.0)
+    sums = [jnp.sum(jnp.where(part == 4 + n, total, 0.0), axis=1, keepdims=True) for n in range(4)]
+    across_bands = [jnp.sum(jnp.where(part // 2 == k, total, 0.0), axis=1, keepdims=True) for k in range(2)]
+
+    def by_component(pair, n):
+        return jnp.where(lane[:1] < LANES // 2, pair[0][n : n + 1], pair[1][n : n + 1])
+
+    none = jnp.zeros((1, LANES), jnp.float32)
+    cross_lines = [none] + [by_component(across_bands, m) for m in range(1, REACH + 1)]
     gram = {}
     for n, pair in enumerate(PAIRS):
-        line = [quarters[2 * k + n // 8][n % 8 : n % 8 + 1] for k in range(2)]
-        gram[pair] = jnp.where(lane[:1] < LANES // 2, line[0], line[1])
-        degree = sum(pair)
-        if degree:
-            gram[pair] = gram[pair] + halves[degree]
-        if pair[0] % 2 and pair[1] % 2:
-            gram[pair] = gram[pair] + SCALE * (SHIFTS[1] - SHIFTS[0]) * halves[degree - 1]
+        own_line = by_component((sums[n // 8], sums[2 + n // 8]), n % 8)
+        gram[pair] = own_line + crossed(pair, cross_lines)
     found = coefficients(gram)
     for k in range(2):
         weights = [value[:, k * LANES // 2 : k * LANES // 2 + 1] for value in found]
@@ -575,8 +578,8 @@
             pltpu.VMEM((2, ITERS + 1, tiles, wide, LANES), jnp.float32),
             pltpu.VMEM((2, REACH - ITERS, tiles, 2 * EDGE, LANES), jnp.float32),
             pltpu.VMEM((2, ITERS, tiles, wide, LANES), jnp.float32),
-            pltpu.VMEM((16, LANES), jnp.float32),
-            pltpu.VMEM((bands, 16, LANES), jnp.float32),
+            pltpu.VMEM((8, LANES), jnp.float32),
+            pltpu.VMEM((bands, 8, LANES), jnp.float32),
             pltpu.SemaphoreType.DMA((2, chunks)),
             pltpu.SemaphoreType.DMA((5,)),
             pltpu.SemaphoreType.DMA((chunks,)),

time: 46.1 us -> 46 us (level)
  no operation moved by 1% of the time
where the time goes in v6:
time: 46 us; the launch traced here: 45.9 us
  Pallas kernels  45.1 us (98%)
  local copies, waits for them, and re-layouts  0.71 us (2%)
    pallas_call x1, Pallas kernels, per_device(): pl.pallas_call(functools.partial(kernel, sections, bands), out_shape=jax....  45.1 us

profile of v6, /device:TPU:248, one launch (start us, length us, event | category | flops | bytes accessed | tf_op | source)
XLA Modules:
  0.0 45.9 jit_solution(12220146182979415807)
XLA Ops:
  0.0 45.1 %shard_map.73 = f32[2,32,1024]{2,1,0:T(8,128)S(1)} custom-call(bf16[1,128,4096]{2,1,0:T(8,128)(2,1)} %image_hbm.1, s32[1,128,4096]{2,1,0:T(8,128)} %mask_hbm.1, f32[1,32,1024]{2,1,0:T(8,128)} %anchor_hbm.1, s32[1,32,1024]{2,1,0:T(8,128)} %fixed_hbm.1, f32[2,1,32,1024]{3,2,1,0:T(8,128)} %prior_hbm.1, bf16[256,256]{1,0:T(8,128)(2,1)} %constant.4.clone.both_hbm, ...), custom_call_target="tpu_custom_call" | custom-call | flops 2400000000 | bytes 4000000 | tf_op jit(solution)/shard_map/pallas_call | solution.py:550
  45.1 0.7 %copy.10 = f32[2,1,32,1024]{3,2,1,0:T(8,128)} copy(f32[2,1,32,1024]{3,2,1,0:T(8,128)S(1)} %bitcast.3) | data formatting | bytes 524288

commit v7 on v6

--- a/solution.py
+++ b/solution.py
@@ -18,6 +18,8 @@
 EDGE = 8
 SPAN = 4
 REACH = 2 * ITERS - 1
+GROUP = 4
+ASIDE = 10
 SHIFTS = (1.0, 4.0, 1.0, 4.0, 1.0, 4.0, 1.0)
 SCALE = 0.25
 PAIRS = tuple((i, j) for i in range(ITERS) for j in range(i, ITERS)) + tuple((i, ITERS) for i in range(ITERS))
@@ -136,6 +138,7 @@
     mask,
     masked,
     arrived,
+    relay,
     spectra,
     both,
     narrow,
@@ -170,6 +173,8 @@
     share_send,
     share_recv,
     round_sem,
+    relay_recv,
+    relay_send,
 ):
     chunks = image.shape[0]
     tiles = pull.shape[0]
@@ -191,6 +196,14 @@
     )
     others = [moved(*step) for step in steps if any(step)]
 
+    group, groups = sec // GROUP, sections // GROUP
+    place = lax.rem(sec, GROUP)
+    gives = (place == 0) & (group > 0)
+    passes = (place == 0) & (group < groups - 1)
+    takes = (place == GROUP - 1) & (group < groups - 1)
+    aside = jnp.where(gives, jnp.minimum(2 * (groups - group), ASIDE), 0)
+    passing = jnp.where(passes, jnp.minimum(2 * (groups - 1 - group), ASIDE), 0)
+
     def pixels(c):
         return pl.ds(pl.multiple_of(c * PAIR, PAIR), PAIR)
 
@@ -204,6 +217,39 @@
         return pltpu.make_async_remote_copy(
             masked.at[c], arrived.at[c], send_sem.at[c], recv_sem.at[c], device_id={"sec": sec - 1}, device_id_type=MESH
         )
+
+    def sent_aside(c):
+        slot = c - (chunks - aside)
+        return pltpu.make_async_remote_copy(
+            masked.at[c],
+            relay.at[slot],
+            send_sem.at[c],
+            relay_recv.at[slot],
+            device_id={"sec": sec - GROUP},
+            device_id_type=MESH,
+        )
+
+    def passed_on(slot):
+        c = chunks - passing + slot
+        return pltpu.make_async_remote_copy(
+            relay.at[slot],
+            arrived.at[c],
+            relay_send.at[slot],
+            recv_sem.at[c],
+            device_id={"sec": sec + GROUP - 1},
+            device_id_type=MESH,
+        )
+
+    def pass_on(slot):
+        pltpu.make_async_remote_copy(
+            masked.at[slot],
+            relay.at[slot],
+            send_sem.at[slot],
+            relay_recv.at[slot],
+            device_id={"sec": sec + GROUP},
+            device_id_type=MESH,
+        ).wait_recv()
+        passed_on(slot).start()
 
     mesh_loads = [
         pltpu.make_async_copy(both_hbm, both, mesh_sem.at[0]),
@@ -220,6 +266,10 @@
 
     pl.when(has_prev)(lambda: greet({"sec": sec - 1}))
     pl.when(has_next)(lambda: greet({"sec": sec + 1}))
+    pl.when(gives)(lambda: greet({"sec": sec - GROUP}))
+    pl.when(passes)(lambda: greet({"sec": sec + GROUP}))
+    pl.when(passes)(lambda: greet({"sec": sec + GROUP - 1}))
+    pl.when(takes)(lambda: greet({"sec": sec - GROUP + 1}))
     pl.when(has_above)(lambda: greet({"blk": blk - 1}))
     pl.when(has_below)(lambda: greet({"blk": blk + 1}))
     across, over = moved(0, 0, 1), moved(0, 1, 0)
@@ -244,7 +294,9 @@
 
     def hide_and_send(c, _):
         hide(c)
-        pl.when(has_prev)(lambda: sent(c).start())
+        straight = c < chunks - aside
+        pl.when(has_prev & straight)(lambda: sent(c).start())
+        pl.when(has_prev & jnp.logical_not(straight))(lambda: sent_aside(c).start())
         return 0
 
     hide(0)
@@ -293,7 +345,7 @@
 
     edge_up[...] = packed(0, EDGE)
     edge_down[...] = packed(rows - SPAN, SPAN)
-    greeted = has_prev, has_next, has_above, has_below
+    greeted = has_prev, has_next, has_above, has_below, gives, passes, passes, takes
     pl.semaphore_wait(barrier, turns + 1 + functools.reduce(lambda p, q: p + q, [g.astype(jnp.int32) for g in greeted]))
     pl.when(has_above)(lambda: edge_copy(True).start())
     pl.when(has_below)(lambda: edge_copy(False).start())
@@ -342,6 +394,7 @@
 
     def correlate(c, _):
         sent(c).wait_recv()
+        pl.when(c < passing)(lambda: pass_on(c))
         other = spectrum(arrived[c], narrow[...], both[...])
         for k, value in enumerate(flows_of(spectra[c], other, narrow[...], both[...])):
             held = flow[k]
@@ -536,6 +589,12 @@
     def _():
         lax.fori_loop(0, chunks, drain, 0)
 
+    def drain_passed(slot, _):
+        passed_on(slot).wait_send()
+        return 0
+
+    lax.fori_loop(0, passing, drain_passed, 0)
+
 
 def per_device(sections, bands, image, tissue_mask, anchor, fixed_nodes, prior_shift):
     _, size, columns = image.shape
@@ -557,6 +616,7 @@
             pltpu.VMEM((chunks, size, PAIR), jnp.int32),
             pltpu.VMEM((chunks, size, PAIR), jnp.bfloat16),
             pltpu.VMEM((chunks, size, PAIR), jnp.bfloat16),
+            pltpu.VMEM((ASIDE, size, PAIR), jnp.bfloat16),
             pltpu.VMEM((chunks, PAIR, PAIR), jnp.bfloat16),
             pltpu.VMEM((PAIR, PAIR), jnp.bfloat16),
             pltpu.VMEM((PAIR, SIZE), jnp.bfloat16),
@@ -591,6 +651,8 @@
             pltpu.SemaphoreType.DMA((bands - 1,)),
             pltpu.SemaphoreType.DMA((bands - 1,)),
             pltpu.SemaphoreType.REGULAR((2,)),
+            pltpu.SemaphoreType.DMA((ASIDE,)),
+            pltpu.SemaphoreType.DMA((ASIDE,)),
         ],
         compiler_params=pltpu.CompilerParams(
             collective_id=0, has_side_effects=True, vmem_limit_bytes=40 * 1024 * 1024

time: 46 us -> 44.3 us (0.963)
  the two profiles are of different devices: /device:TPU:248 before, /device:TPU:208 now
where the time goes in v7:
time: 44.3 us; the launch traced here: 44.2 us
  Pallas kernels  43.4 us (98%)
  local copies, waits for them, and re-layouts  0.71 us (2%)
    pallas_call x1, Pallas kernels, per_device(): pl.pallas_call(functools.partial(kernel, sections, bands), out_shape=jax....  43.4 us

profile of v7, /device:TPU:208, one launch (start us, length us, event | category | flops | bytes accessed | tf_op | source)
XLA Modules:
  0.0 44.2 jit_solution(4609176749711062356)
XLA Ops:
  0.0 43.4 %shard_map.73 = f32[2,32,1024]{2,1,0:T(8,128)S(1)} custom-call(bf16[1,128,4096]{2,1,0:T(8,128)(2,1)} %image_hbm.1, s32[1,128,4096]{2,1,0:T(8,128)} %mask_hbm.1, f32[1,32,1024]{2,1,0:T(8,128)} %anchor_hbm.1, s32[1,32,1024]{2,1,0:T(8,128)} %fixed_hbm.1, f32[2,1,32,1024]{3,2,1,0:T(8,128)} %prior_hbm.1, bf16[256,256]{1,0:T(8,128)(2,1)} %constant.4.clone.both_hbm, ...), custom_call_target="tpu_custom_call" | custom-call | flops 2400000000 | bytes 4000000 | tf_op jit(solution)/shard_map/pallas_call | solution.py:609
  43.4 0.7 %copy.10 = f32[2,1,32,1024]{3,2,1,0:T(8,128)} copy(f32[2,1,32,1024]{3,2,1,0:T(8,128)S(1)} %bitcast.3) | data formatting | bytes 524288

commit v8 on v7

--- a/solution.py
+++ b/solution.py
@@ -149,6 +149,8 @@
     edge_down,
     from_below,
     from_above,
+    via_up,
+    via_down,
     pull,
     diag,
     link,
@@ -175,6 +177,8 @@
     round_sem,
     relay_recv,
     relay_send,
+    via_recv,
+    via_send,
 ):
     chunks = image.shape[0]
     tiles = pull.shape[0]
@@ -264,17 +268,17 @@
     def greet(device):
         pl.semaphore_signal(barrier, inc=1, device_id=device, device_id_type=MESH)
 
+    across, over, facing = moved(0, 0, 1), moved(0, 1, 0), moved(0, 1, 1)
+    along = [moved(dx, 0, 0) for dx in range(1, turns)]
+    greet({"blk": facing})
+    greet({"blk": over})
     pl.when(has_prev)(lambda: greet({"sec": sec - 1}))
     pl.when(has_next)(lambda: greet({"sec": sec + 1}))
+    pl.when(passes)(lambda: greet({"sec": sec + GROUP - 1}))
+    pl.when(takes)(lambda: greet({"sec": sec - GROUP + 1}))
     pl.when(gives)(lambda: greet({"sec": sec - GROUP}))
     pl.when(passes)(lambda: greet({"sec": sec + GROUP}))
-    pl.when(passes)(lambda: greet({"sec": sec + GROUP - 1}))
-    pl.when(takes)(lambda: greet({"sec": sec - GROUP + 1}))
-    pl.when(has_above)(lambda: greet({"blk": blk - 1}))
-    pl.when(has_below)(lambda: greet({"blk": blk + 1}))
-    across, over = moved(0, 0, 1), moved(0, 1, 0)
-    along = [moved(dx, 0, 0) for dx in range(1, turns)]
-    for other in [across, over] + along:
+    for other in along + [across]:
         greet({"blk": other})
 
     def start_loads(c, _):
@@ -317,6 +321,28 @@
             device_id_type=MESH,
         )
 
+    def edge_via(up):
+        slot = 0 if up else 1
+        return pltpu.make_async_remote_copy(
+            edge_up if up else edge_down,
+            via_up if up else via_down,
+            edge_send.at[slot],
+            via_recv.at[slot],
+            device_id={"blk": facing},
+            device_id_type=MESH,
+        )
+
+    def edge_onward(up):
+        slot = 0 if up else 1
+        return pltpu.make_async_remote_copy(
+            via_up if up else via_down,
+            from_below if up else from_above,
+            via_send.at[slot],
+            edge_recv.at[slot],
+            device_id={"blk": blk - 4 if up else blk + 4},
+            device_id_type=MESH,
+        )
+
     def flow_copy(up):
         slot = 0 if up else 1
         return pltpu.make_async_remote_copy(
@@ -345,10 +371,14 @@
 
     edge_up[...] = packed(0, EDGE)
     edge_down[...] = packed(rows - SPAN, SPAN)
-    greeted = has_prev, has_next, has_above, has_below, gives, passes, passes, takes
-    pl.semaphore_wait(barrier, turns + 1 + functools.reduce(lambda p, q: p + q, [g.astype(jnp.int32) for g in greeted]))
-    pl.when(has_above)(lambda: edge_copy(True).start())
-    pl.when(has_below)(lambda: edge_copy(False).start())
+    greeted = has_prev, has_next, gives, passes, passes, takes
+    pl.semaphore_wait(barrier, turns + 2 + functools.reduce(lambda p, q: p + q, [g.astype(jnp.int32) for g in greeted]))
+    lowest = (here[1] == 0) & (here[2] == 0)
+    highest = (here[1] == 1) & (here[2] == 1)
+    pl.when(has_above & jnp.logical_not(lowest))(lambda: edge_copy(True).start())
+    pl.when(has_below & jnp.logical_not(highest))(lambda: edge_copy(False).start())
+    pl.when(has_above & lowest)(lambda: edge_via(True).start())
+    pl.when(has_below & highest)(lambda: edge_via(False).start())
     pl.when(has_prev)(lambda: sent(0).start())
     pl.semaphore_signal(round_sem.at[0], inc=1, device_id={"blk": across}, device_id_type=MESH)
     lax.fori_loop(1, 8, hide_and_send, 0)
@@ -361,6 +391,19 @@
         return 0
 
     lax.fori_loop(0, chunks, own_spectrum, 0)
+    onward_up = highest & (here[0] > 0)
+    onward_down = lowest & (here[0] < turns - 1)
+
+    @pl.when(onward_up)
+    def _():
+        edge_via(True).wait_recv()
+        edge_onward(True).start()
+
+    @pl.when(onward_down)
+    def _():
+        edge_via(False).wait_recv()
+        edge_onward(False).start()
+
     pl.semaphore_wait(round_sem.at[1], 1)
 
     pull[...] = jnp.zeros_like(pull)
@@ -513,6 +556,30 @@
         share_copy(n).start()
     shares[blk] = share[...]
 
+    def drain(c, _):
+        sent(c).wait_send()
+        return 0
+
+    def drain_passed(slot, _):
+        passed_on(slot).wait_send()
+        return 0
+
+    @pl.when(has_prev)
+    def _():
+        lax.fori_loop(0, chunks, drain, 0)
+
+    lax.fori_loop(0, passing, drain_passed, 0)
+    pl.when(onward_up)(lambda: edge_onward(True).wait_send())
+    pl.when(onward_down)(lambda: edge_onward(False).wait_send())
+
+    @pl.when(has_above)
+    def _():
+        edge_copy(True).wait_send()
+
+    @pl.when(has_below)
+    def _():
+        edge_copy(False).wait_send()
+
     @pl.when(has_below)
     def _():
         flow_copy(True).wait_recv()
@@ -541,7 +608,15 @@
         for step in range(ITERS - 1):
             whole[k, step + 1] = advance(whole[k, step], step)
 
-    for n in range(bands - 1):
+    @pl.when(has_above)
+    def _():
+        flow_copy(True).wait_send()
+
+    @pl.when(has_below)
+    def _():
+        flow_copy(False).wait_send()
+
+    for n in reversed(range(bands - 1)):
         share_copy(n).wait_recv()
     total = shares[bands - 1]
     for n in range(bands - 1):
@@ -570,30 +645,6 @@
 
     for n in range(bands - 1):
         share_copy(n).wait_send()
-
-    @pl.when(has_above)
-    def _():
-        edge_copy(True).wait_send()
-        flow_copy(True).wait_send()
-
-    @pl.when(has_below)
-    def _():
-        edge_copy(False).wait_send()
-        flow_copy(False).wait_send()
-
-    def drain(c, _):
-        sent(c).wait_send()
-        return 0
-
-    @pl.when(has_prev)
-    def _():
-        lax.fori_loop(0, chunks, drain, 0)
-
-    def drain_passed(slot, _):
-        passed_on(slot).wait_send()
-        return 0
-
-    lax.fori_loop(0, passing, drain_passed, 0)
 
 
 def per_device(sections, bands, image, tissue_mask, anchor, fixed_nodes, prior_shift):
@@ -627,6 +678,8 @@
             pltpu.VMEM((4 * SPAN, width), jnp.bfloat16),
             pltpu.VMEM((4 * SPAN, 2 * width), jnp.bfloat16),
             pltpu.VMEM((4 * SPAN, width), jnp.bfloat16),
+            pltpu.VMEM((4 * SPAN, 2 * width), jnp.bfloat16),
+            pltpu.VMEM((4 * SPAN, width), jnp.bfloat16),
             pltpu.VMEM((tiles, wide, LANES), jnp.float32),
             pltpu.VMEM((tiles, wide, LANES), jnp.float32),
             pltpu.VMEM((tiles, wide, LANES), jnp.float32),
@@ -653,6 +706,8 @@
             pltpu.SemaphoreType.REGULAR((2,)),
             pltpu.SemaphoreType.DMA((ASIDE,)),
             pltpu.SemaphoreType.DMA((ASIDE,)),
+            pltpu.SemaphoreType.DMA((2,)),
+            pltpu.SemaphoreType.DMA((2,)),
         ],
         compiler_params=pltpu.CompilerParams(
             collective_id=0, has_side_effects=True, vmem_limit_bytes=40 * 1024 * 1024

time: 44.3 us -> 44.2 us (level)
  no operation moved by 1% of the time
where the time goes in v8:
time: 44.2 us; the launch traced here: 44 us
  Pallas kernels  43.3 us (98%)
  local copies, waits for them, and re-layouts  0.71 us (2%)
    pallas_call x1, Pallas kernels, per_device(): pl.pallas_call(functools.partial(kernel, sections, bands), out_shape=jax....  43.3 us

profile of v8, /device:TPU:208, one launch (start us, length us, event | category | flops | bytes accessed | tf_op | source)
XLA Modules:
  0.0 44.0 jit_solution(2416656738020567577)
XLA Ops:
  0.0 43.3 %shard_map.73 = f32[2,32,1024]{2,1,0:T(8,128)S(1)} custom-call(bf16[1,128,4096]{2,1,0:T(8,128)(2,1)} %image_hbm.1, s32[1,128,4096]{2,1,0:T(8,128)} %mask_hbm.1, f32[1,32,1024]{2,1,0:T(8,128)} %anchor_hbm.1, s32[1,32,1024]{2,1,0:T(8,128)} %fixed_hbm.1, f32[2,1,32,1024]{3,2,1,0:T(8,128)} %prior_hbm.1, bf16[256,256]{1,0:T(8,128)(2,1)} %constant.4.clone.both_hbm, ...), custom_call_target="tpu_custom_call" | custom-call | flops 2400000000 | bytes 4000000 | tf_op jit(solution)/shard_map/pallas_call | solution.py:660
  43.3 0.7 %copy.10 = f32[2,1,32,1024]{3,2,1,0:T(8,128)} copy(f32[2,1,32,1024]{3,2,1,0:T(8,128)S(1)} %bitcast.3) | data formatting | bytes 524288

commit v9 on v8

--- a/solution.py
+++ b/solution.py
@@ -19,7 +19,7 @@
 SPAN = 4
 REACH = 2 * ITERS - 1
 GROUP = 4
-ASIDE = 10
+ASIDE = 8
 SHIFTS = (1.0, 4.0, 1.0, 4.0, 1.0, 4.0, 1.0)
 SCALE = 0.25
 PAIRS = tuple((i, j) for i in range(ITERS) for j in range(i, ITERS)) + tuple((i, ITERS) for i in range(ITERS))

time: 44.2 us -> 44.1 us (level)
  the two profiles are of different devices: /device:TPU:208 before, /device:TPU:209 now
where the time goes in v9:
time: 44.1 us; the launch traced here: 43.9 us
  Pallas kernels  43.2 us (98%)
  local copies, waits for them, and re-layouts  0.71 us (2%)
    pallas_call x1, Pallas kernels, per_device(): pl.pallas_call(functools.partial(kernel, sections, bands), out_shape=jax....  43.2 us

profile of v9, /device:TPU:209, one launch (start us, length us, event | category | flops | bytes accessed | tf_op | source)
XLA Modules:
  0.0 43.9 jit_solution(13121551961068984439)
XLA Ops:
  0.0 43.2 %shard_map.73 = f32[2,32,1024]{2,1,0:T(8,128)S(1)} custom-call(bf16[1,128,4096]{2,1,0:T(8,128)(2,1)} %image_hbm.1, s32[1,128,4096]{2,1,0:T(8,128)} %mask_hbm.1, f32[1,32,1024]{2,1,0:T(8,128)} %anchor_hbm.1, s32[1,32,1024]{2,1,0:T(8,128)} %fixed_hbm.1, f32[2,1,32,1024]{3,2,1,0:T(8,128)} %prior_hbm.1, bf16[256,256]{1,0:T(8,128)(2,1)} %constant.4.clone.both_hbm, ...), custom_call_target="tpu_custom_call" | custom-call | flops 2400000000 | bytes 4000000 | tf_op jit(solution)/shard_map/pallas_call | solution.py:660
  43.2 0.7 %copy.10 = f32[2,1,32,1024]{3,2,1,0:T(8,128)} copy(f32[2,1,32,1024]{3,2,1,0:T(8,128)S(1)} %bitcast.3) | data formatting | bytes 524288
